TPU v7x, 256 devices: a whole 4x4x8 slice. The times are simulated.
256 devices in a mesh: fsdp: 64 (over y, z_lo, x), dp: 4 (over z_hi, core).
Axes of the slice: x: 4, y: 4, z: 8 (z_hi: 2, z_lo: 4; z = z_hi * 4 + z_lo), core: 2. Of those that a mesh axis runs over, the one named last changes fastest.
Arguments:
- tokens: bfloat16 [32768, 2048], P(('fsdp', 'dp')), may hold values from -24 to 24
- cotangent: bfloat16 [32768, 2048], P(('fsdp', 'dp')), may hold values from -0.099121094 to 0.099121094
- saved_branch: bfloat16 [32768, 2048], P(('fsdp', 'dp')), may hold values from -6 to 6
- layer_gain: float32 [2048], replicated, may hold values from -3 to 3
- offsets: int32 [3], replicated, may hold values from 0 to 4225024, as said below
- master: float32 [4227072], P('fsdp'), may hold values from -0.006 to 0.006
- moment_one: float32 [4227072], P('fsdp'), may hold values from -6 to 6
- moment_two: float32 [4227072], P('fsdp'), may hold values from 0.5 to 20
- teacher: float32 [4227072], P('fsdp'), may hold values from -0.00012 to 0.00012
- teacher_tokens: bfloat16 [32768, 2048], P(('fsdp', 'dp')), may hold values from -6 to 6
Outputs:
- master_new: float32 [4227072], P('fsdp')
- moment_one_new: float32 [4227072], P('fsdp')
- moment_two_new: float32 [4227072], P('fsdp')
- teacher_new: float32 [4227072], P('fsdp')
- teacher_branch: bfloat16 [32768, 2048], P(('fsdp', 'dp'))
Inputs may be any that keep to these rules, and one draw needn't show every extreme that they name: offsets[0] = 0; the projection (4194304 slots), the bias (2048) and the layer scale (2048) lie in that order without intersection, the layer scale at the bucket's end.
All inputs are finite; a program needn't handle non-finite values.
Results may differ from a plain program's by a relative error of at most 0.0056.
Values may be sent and summed in bfloat16 or wider, within the bound.
A program may use at most 128 MiB of HBM per device.

v0:
```python
import jax
import jax.numpy as jnp
from jax import lax
from jax.sharding import PartitionSpec as P

STEP = 1000


beta_one = 0.9
beta_two = 0.999
learn_rate = 0.001
decay_rate = 0.04
ema_rate = 0.994
epsilon = 1e-08


def per_device(
    tokens,
    cotangent,
    saved_branch,
    layer_gain,
    offsets,
    master,
    moment_one,
    moment_two,
    teacher,
    teacher_tokens,
):
    width_in = tokens.shape[1]
    width_out = cotangent.shape[1]
    groups = lax.axis_size("fsdp")
    shard = master.shape[0]
    total = shard * groups
    cot_float = cotangent.astype(jnp.float32)
    scaled = cot_float * layer_gain
    weighted = scaled.astype(jnp.bfloat16)
    grad_proj = lax.dot_general(
        tokens, weighted, (((0,), (0,)), ((), ())), preferred_element_type=jnp.float32
    )
    grad_bias = jnp.sum(scaled, axis=0)
    grad_scale = jnp.sum(cot_float * saved_branch.astype(jnp.float32), axis=0)
    start_proj = offsets[0]
    start_bias = offsets[1]
    start_scale = offsets[2]
    flat = jnp.zeros((total,), jnp.float32)
    flat = lax.dynamic_update_slice(flat, grad_proj.reshape(-1), (start_proj,))
    flat = lax.dynamic_update_slice(flat, grad_bias, (start_bias,))
    flat = lax.dynamic_update_slice(flat, grad_scale, (start_scale,))
    summed_block = lax.psum_scatter(flat, ("fsdp", "dp"), scatter_dimension=0, tiled=True)
    grad = lax.all_gather(summed_block, "dp", axis=0, tiled=True)
    moment_one_new = beta_one * moment_one + (1.0 - beta_one) * grad
    moment_two_new = beta_two * moment_two + (1.0 - beta_two) * grad * grad
    first = moment_one_new / (1.0 - beta_one**STEP)
    second = moment_two_new / (1.0 - beta_two**STEP)
    places = lax.axis_index("fsdp") * shard + jnp.arange(shard, dtype=jnp.int32)
    inside = jnp.logical_and(places >= start_proj, places < start_proj + width_in * width_out)
    mask = jnp.where(inside, 1.0, 0.0).astype(jnp.float32)
    master_new = master - learn_rate * (
        first / (jnp.sqrt(second) + epsilon) + decay_rate * mask * master
    )
    teacher_new = ema_rate * teacher + (1.0 - ema_rate) * master_new
    teacher_low = teacher_new.astype(jnp.bfloat16)
    gathered = lax.all_gather(teacher_low, "fsdp", axis=0, tiled=True)
    proj_t = lax.dynamic_slice(gathered, (start_proj,), (width_in * width_out,)).reshape(
        width_in, width_out
    )
    bias_t = lax.dynamic_slice(gathered, (start_bias,), (width_out,)).astype(jnp.float32)
    scale_t = lax.dynamic_slice(gathered, (start_scale,), (width_out,)).astype(jnp.float32)
    product = jnp.dot(teacher_tokens, proj_t, preferred_element_type=jnp.float32)
    teacher_branch = (scale_t * (product + bias_t)).astype(jnp.bfloat16)
    return (master_new, moment_one_new, moment_two_new, teacher_new, teacher_branch)


def solution(mesh):
    return jax.shard_map(
        per_device,
        mesh=mesh,
        in_specs=(
            P(("fsdp", "dp"), None),
            P(("fsdp", "dp"), None),
            P(("fsdp", "dp"), None),
            P(),
            P(),
            P("fsdp"),
            P("fsdp"),
            P("fsdp"),
            P("fsdp"),
            P(("fsdp", "dp"), None),
        ),
        out_specs=(P("fsdp"), P("fsdp"), P("fsdp"), P("fsdp"), P(("fsdp", "dp"), None)),
        check_vma=False,
    )
```

profile of v0, /device:TPU:2, one launch (start us, length us, event | category | flops | bytes accessed | tf_op | source)
XLA Modules:
  0.0 1001.6 jit_solution(1658165034310731052)
XLA Ops:
  7.2 0.0 copy-start
  7.2 0.0 all-reduce.3.cloned.1.call-start
  7.2 1.4 fusion.14
  12.5 0.0 copy-done
  12.5 9.1 convolution_bitcast_fusion
  21.6 17.6 %copy.18 = f32[2048,2048]{1,0:T(8,128)} copy(f32[2048,2048]{0,1:T(8,128)} %convolution_bitcast_fusion) | data formatting | bytes 33554432 | tf_op jit(solution)/shard_map/dot_general | solution.py:37
  39.2 0.0 copy-start.2
  39.2 0.0 copy-start.3
  39.2 0.0 copy-start.8
  39.2 14.2 %copy.20 = f32[256,16,8,128]{3,1,2,0:T(8,128)} copy(f32[256,16,8,128]{3,2,1,0:T(8,128)} %bitcast.13) | data formatting | bytes 33554432
  53.4 0.0 copy-done.2
  53.4 0.0 copy-done.3
  53.4 0.0 copy-done.8
  53.4 0.2 fusion.5
  55.6 6.0 broadcast_in_dim.12
  61.6 141.6 %dynamic_update_slice.9 = f32[4227072]{0:T(1024)} dynamic-update-slice(f32[4227072]{0:T(1024)} %broadcast_in_dim.12, f32[4194304]{0:T(1024)} %bitcast.12, s32[]{:T(128)S(6)} %select_n.16) | dynamic-update-slice | bytes 33554436 | tf_op jit(solution)/shard_map/dynamic_update_slice | solution.py:46
  203.1 0.0 copy-start.4
  203.1 0.0 copy-start.5
  203.1 0.0 copy-start.6
  203.2 0.0 copy-start.7
  203.2 1.5 dynamic_update_slice.10
  204.7 1.4 dynamic_update_slice.11
  206.1 0.0 all-reduce.3.cloned.1.call-update
  206.1 0.0 all-gather.4.cloned.1.call-start
  206.8 299.4 %all-reduce.3.cloned.1.call-done = f32[4227072]{0:T(1024)} async-done(((f32[4227072]{0:T(1024)}), f32[4227072]{0:T(1024)}) %all-reduce.3.cloned.1.call-update) | async-done | bytes 16908304
  506.2 1.0 dynamic-slice
  507.2 10.5 %all-gather = f32[4,1,16512]{2,1,0:T(1,128)S(1)} all-gather(f32[1,1,16512]{2,1,0:T(1,128)S(1)} %reshape.21), channel_id=1, replica_groups=mesh['fsdp'=64,'dp'=4] {'dp'}, dimensions={0}, use_global_device_ids=true | all-gather | bytes 330240 | tf_op jit(solution)/shard_map/all_gather | solution.py:50
  517.7 0.7 reduce
  518.5 0.1 reshape.22
  518.6 0.0 copy-done.4
  518.6 0.0 copy-done.5
  518.6 0.0 copy-done.6
  518.6 0.0 copy-done.7
  518.6 1.8 fusion.12
  520.5 0.8 reshape.23
  521.3 0.0 all-gather.4.cloned.1.call-update
  521.3 377.6 %all-gather.4.cloned.1.call-done = bf16[64,1,66048]{2,1,0:T(2,128)(2,1)} async-done(((bf16[1,1,66048]{2,1,0:T(2,128)(2,1)}), bf16[64,1,66048]{2,1,0:T(2,128)(2,1)}) %all-gather.4.cloned.1.call-update) | async-done | bytes 8454160 | tf_op jit(solution)/shard_map/all_gather | solution.py:63
  898.9 50.2 %reduce.1 = bf16[64,66048]{1,0:T(8,128)(2,1)} reduce(bf16[64,1,66048]{2,1,0:T(2,128)(2,1)} %all-gather.4.cloned.1.call-done, bf16[]{:T(256)} %constant.47), dimensions={1}, to_apply=%all-gather.1.reduce_sub_computation | reduce | bytes 16908290 | tf_op jit(solution)/shard_map/all_gather | solution.py:63
  949.1 15.1 %reshape.24 = bf16[4227072]{0:T(1024)(128)(2,1)} reshape(bf16[64,66048]{1,0:T(8,128)(2,1)} %reduce.1) | data formatting | bytes 16908288
  964.2 0.8 dynamic-slice_convert_fusion.1
  964.9 0.0 copy-start.9
  964.9 0.0 copy-start.1
  964.9 9.3 dynamic_slice.10
  974.3 13.3 %reshape.20 = bf16[2048,2048]{1,0:T(8,128)(2,1)} reshape(bf16[4194304]{0:T(1024)(128)(2,1)} %dynamic_slice.10) | data formatting | bytes 16777216 | tf_op jit(solution)/shard_map/reshape | solution.py:64
  987.6 0.0 copy-done.9
  987.6 6.2 fusion.2
  993.8 1.0 copy.19
  994.8 0.0 copy-done.1
  (1 shorter events, 0.0 us)
Async XLA Ops:
  7.2 5.3 copy-start
  7.2 499.0 %all-reduce.3.cloned.1.call-start = ((), (), s32[]{:S(2)}) async-start(), calls=%async_computation.1 | async-start | bytes 33816576
  39.2 14.2 %copy-start.2 = (bf16[128,2048]{1,0:T(8,128)(2,1)S(1)}, bf16[128,2048]{1,0:T(8,128)(2,1)}, u32[]{:S(2)}) copy-start(bf16[128,2048]{1,0:T(8,128)(2,1)} %param.11) | copy-start | bytes 1572868
  39.2 14.2 %copy-start.3 = (bf16[128,2048]{1,0:T(8,128)(2,1)S(1)}, bf16[128,2048]{1,0:T(8,128)(2,1)}, u32[]{:S(2)}) copy-start(bf16[128,2048]{1,0:T(8,128)(2,1)} %param.12) | copy-start | bytes 1572868
  39.2 14.2 %copy-start.8 = (f32[2048]{0:T(1024)S(1)}, f32[2048]{0:T(1024)}, u32[]{:S(2)}) copy-start(f32[2048]{0:T(1024)} %param.13) | copy-start | bytes 24580
  203.1 315.5 %copy-start.4 = (f32[66048]{0:T(1024)S(1)}, f32[66048]{0:T(1024)}, u32[]{:S(2)}) copy-start(f32[66048]{0:T(1024)} %param.18) | copy-start | bytes 792580
  203.1 315.5 %copy-start.5 = (f32[66048]{0:T(1024)S(1)}, f32[66048]{0:T(1024)}, u32[]{:S(2)}) copy-start(f32[66048]{0:T(1024)} %param.15) | copy-start | bytes 792580
  203.1 315.5 %copy-start.6 = (f32[66048]{0:T(1024)S(1)}, f32[66048]{0:T(1024)}, u32[]{:S(2)}) copy-start(f32[66048]{0:T(1024)} %param.17) | copy-start | bytes 792580
  203.2 315.5 %copy-start.7 = (f32[66048]{0:T(1024)S(1)}, f32[66048]{0:T(1024)}, u32[]{:S(2)}) copy-start(f32[66048]{0:T(1024)} %param.16) | copy-start | bytes 792580
  206.1 692.8 %all-gather.4.cloned.1.call-start = ((), (), s32[]{:S(2)}) async-start(), calls=%async_computation | async-start | bytes 17172480 | tf_op jit(solution)/shard_map/all_gather | solution.py:63
  964.9 22.7 %copy-start.9 = (bf16[128,2048]{1,0:T(8,128)(2,1)S(1)}, bf16[128,2048]{1,0:T(8,128)(2,1)}, u32[]{:S(2)}) copy-start(bf16[128,2048]{1,0:T(8,128)(2,1)} %param.19) | copy-start | bytes 1572868
  964.9 29.9 %copy-start.1 = (bf16[128,2048]{1,0:T(8,128)(2,1)S(1)}, bf16[128,2048]{1,0:T(8,128)(2,1)}, u32[]{:S(2)}) copy-start(bf16[128,2048]{1,0:T(8,128)(2,1)} %param.10) | copy-start | bytes 1572868
Sparse Core Ops, SparseCore 0:
  206.2 299.9 all-reduce.2
  521.4 377.4 all-gather.3
where the time goes:
time: 1010 us; the launch traced here: 1000 us
  waiting for transfers between devices  677 us (67%)
  local copies, waits for them, and re-layouts  224 us (22%)
  other arithmetic  53.7 us (5%)
  between operations  20.6 us (2%)
  matrix products  15.3 us (2%)
  blocking collectives  10.5 us (1%)
    all_gather x1, waiting for transfers between devices, per_device(): gathered = lax.all_gather(teacher_low, 'fsdp', axis=0, tiled=True)  378 us
    unnamed x3, waiting for transfers between devices  299 us
    dynamic_update_slice x1, local copies, waits for them, and re-layouts, per_device(): flat = lax.dynamic_update_slice(flat, grad_proj.reshape(-1), (start_proj,))  142 us
    all_gather x1, other arithmetic, per_device(): gathered = lax.all_gather(teacher_low, 'fsdp', axis=0, tiled=True)  50.2 us
    unnamed x27, local copies, waits for them, and re-layouts  32.3 us
  transfers between devices with their start and end apart: 2, of which 2 were waited for; matrix products, arithmetic and copies ran while one was open for 0% of the time, Pallas kernels for 0%

commit v1 on v0

v1 whole, which is shorter than its diff:
```python
import functools

import jax
import jax.numpy as jnp
from jax import lax
from jax.experimental import pallas as pl
from jax.experimental.pallas import tpu as pltpu
from jax.sharding import PartitionSpec as P

MESH = pl.DeviceIdType.MESH
F32 = jnp.float32
BF16 = jnp.bfloat16

STEP = 1000
beta_one = 0.9
beta_two = 0.999
learn_rate = 0.001
decay_rate = 0.04
ema_rate = 0.994
epsilon = 1e-08

WIDTH = 2048
WINDOW = 640
PROJ = WIDTH * WIDTH
SHARD = 66048
FLAT = SHARD // 128
TAIL_ROW = 260


def wrap(value, size):
    return lax.rem(value + size, size)


def device(x, y, z, c):
    return (y * 16 + lax.rem(z, 4) * 4 + x, lax.div(z, 4) * 2 + c)


def window_start(y):
    return pl.multiple_of(jnp.minimum(512 * y, WIDTH - WINDOW), 128)


def remote(src, dst, send, recv, to):
    return pltpu.make_async_remote_copy(
        src_ref=src, dst_ref=dst, send_sem=send, recv_sem=recv, device_id=to, device_id_type=MESH
    )


def bit_of(vector, bit):
    return lax.rem(lax.div(vector, 2**bit), 2) == 1


def roll_by(value, amount, axis, bits):
    for bit in bits:
        on = jnp.broadcast_to(bit_of(amount, bit), value.shape)
        value = jnp.where(on, pltpu.roll(value, 2 ** (bit - bits[0]), axis), value)
    return value


def shift_rows(value, amount):
    for bit in range(3):
        on = lax.rem(lax.div(amount, 2**bit), 2) == 1
        value = jnp.where(on, pltpu.roll(value, value.shape[0] - 2**bit, 0), value)
    return value


def rows_from(ref, start, count):
    base = pl.multiple_of(lax.div(start, 8) * 8, 8)
    return shift_rows(ref[pl.ds(base, count + 8), :], start - base)[:count]


def kernel(
    spot, gain, tokens, cot, saved, master, one, two, teacher,
    master_out, one_out, two_out, teacher_out,
    T, C, SL, SS, prod, zs, cr, zb, zr, xs, xr, pad, tg,
    own_sem, a1s, a1r, b1s, b1r, s1s, s1r, s2s, s2r, a2s, a2r, b2s, b2r, cs, crs, zss, zrs, xss, xrs,
):
    f = lax.axis_index("fsdp")
    p = lax.axis_index("dp")
    x = lax.rem(f, 4)
    zl = lax.rem(lax.div(f, 4), 4)
    y = lax.div(f, 16)
    c = lax.rem(p, 2)
    z = lax.div(p, 2) * 4 + zl

    def at(dx=0, dy=0, dz=0, dc=0):
        return device(wrap(x + dx, 4), wrap(y + dy, 4), wrap(z + dz, 8), wrap(c + dc, 2))

    partners = (
        [dict(dx=d) for d in (1, 2, 3)]
        + [dict(dy=d) for d in (1, 2, 3)]
        + [dict(dz=d) for d in range(1, 8)]
        + [dict(dx=d, dc=1) for d in range(4)]
    )
    barrier = pltpu.get_barrier_semaphore()
    for partner in partners:
        pl.semaphore_signal(barrier, inc=1, device_id=at(**partner), device_id_type=MESH)
    pl.semaphore_wait(barrier, len(partners))

    pending = []

    def send(copy):
        copy.start()
        pending.append(copy)

    mine = [
        pltpu.make_async_copy(tokens.at[:, pl.ds(window_start(y), WINDOW)], T.at[y, x], own_sem.at[0]),
        pltpu.make_async_copy(cot.at[:, pl.ds(pl.multiple_of(512 * x, 128), 512)], C.at[y, x], own_sem.at[1]),
    ]
    for copy in mine:
        copy.start()
    for d in (1, 2, 3):
        to_y = wrap(y + d, 4)
        send(remote(tokens.at[:, pl.ds(window_start(to_y), WINDOW)], T.at[y, x], a1s.at[d - 1], a1r.at[d - 1], at(dy=d)))
        to_x = wrap(x + d, 4)
        send(remote(cot.at[:, pl.ds(pl.multiple_of(512 * to_x, 128), 512)], C.at[y, x], b1s.at[d - 1], b1r.at[d - 1], at(dx=d)))
    for copy in mine:
        copy.wait()

    low, high = pl.ds(0, 64), pl.ds(64, 64)

    def spread_token(d):
        row = wrap(y - d, 4)
        for k, (half, dx) in enumerate([(low, 1), (high, 1), (high, -1), (low, -1)]):
            ref = T.at[row, x, half]
            send(remote(ref, ref, a2s.at[d, k], a2r.at[d, k], at(dx=dx)))

    def spread_cot(d):
        col = wrap(x - d, 4)
        for k, (half, dy) in enumerate([(low, 1), (high, 1), (high, -1), (low, -1)]):
            ref = C.at[y, col, half]
            send(remote(ref, ref, b2s.at[d, k], b2r.at[d, k], at(dy=dy)))

    def token_wait(d, k):
        half, dx = [(low, -1), (high, -1), (high, 1), (low, 1), (low, -2), (high, 2)][k]
        ref = T.at[wrap(y - d, 4), wrap(x + dx, 4), half]
        remote(ref, ref, a2s.at[d, k], a2r.at[d, k], at(dx=1)).wait_recv()
        return ref

    def cot_wait(d, k):
        half, dy = [(low, -1), (high, -1), (high, 1), (low, 1), (low, -2), (high, 2)][k]
        ref = C.at[wrap(y + dy, 4), wrap(x - d, 4), half]
        remote(ref, ref, b2s.at[d, k], b2r.at[d, k], at(dy=1)).wait_recv()
        return ref

    def relay(d):
        ref = token_wait(d, 0)
        send(remote(ref, ref, a2s.at[d, 4], a2r.at[d, 4], at(dx=1)))
        ref = cot_wait(d, 0)
        send(remote(ref, ref, b2s.at[d, 4], b2r.at[d, 4], at(dy=1)))
        ref = token_wait(d, 2)
        send(remote(ref, ref, a2s.at[d, 5], a2r.at[d, 5], at(dx=-1)))
        ref = cot_wait(d, 2)
        send(remote(ref, ref, b2s.at[d, 5], b2r.at[d, 5], at(dy=-1)))

    spread_token(0)
    spread_cot(0)

    total = jnp.zeros((1, WIDTH), F32)
    for r in range(0, 128, 16):
        total += jnp.sum(cot[r : r + 16].astype(F32) * saved[r : r + 16].astype(F32), axis=0, keepdims=True)
    top = total.astype(BF16)
    rest = (total - top.astype(F32)).astype(BF16)
    rows16 = lax.broadcasted_iota(jnp.int32, (16, WIDTH), 0)
    both = jnp.where(rows16 == 0, top.astype(F32), jnp.where(rows16 == 1, rest.astype(F32), 0.0)).astype(BF16)
    for q in range(4):
        SS[q] = both[:, 512 * q : 512 * q + 512]
    for d in (1, 2, 3):
        send(remote(SS.at[wrap(x + d, 4)], SL.at[y, x], s1s.at[d - 1], s1r.at[d - 1], at(dx=d)))
    SL[y, x] = SS[x]

    for d in (1, 2, 3):
        ref = T.at[wrap(y - d, 4), x]
        remote(ref, ref, a1s.at[d - 1], a1r.at[d - 1], at(dy=d)).wait_recv()
        spread_token(d)
        ref = C.at[y, wrap(x - d, 4)]
        remote(ref, ref, b1s.at[d - 1], b1r.at[d - 1], at(dx=d)).wait_recv()
        spread_cot(d)
        relay(d - 1)
    for d in (1, 2, 3):
        ref = SL.at[y, wrap(x - d, 4)]
        remote(ref, ref, s1s.at[d - 1], s1r.at[d - 1], at(dx=d)).wait_recv()
    for d in (1, 2, 3):
        send(remote(SL.at[y], SL.at[y], s2s.at[d - 1], s2r.at[d - 1], at(dy=d)))
    relay(3)
    for d in range(4):
        for k in (1, 3, 4, 5):
            token_wait(d, k)
            cot_wait(d, k)
    for d in (1, 2, 3):
        ref = SL.at[wrap(y - d, 4)]
        remote(ref, ref, s2s.at[d - 1], s2r.at[d - 1], at(dy=d)).wait_recv()

    prod[...] = jnp.zeros_like(prod)
    ones = jnp.ones((16, 512), BF16)

    def multiply(k, sums):
        left = T[k].reshape(512, WINDOW)
        right = C[k].reshape(512, 512)
        prod[0:WINDOW] += lax.dot_general(left, right, (((0,), (0,)), ((), ())), preferred_element_type=F32)
        return sums + jnp.dot(ones, right, preferred_element_type=F32)

    cot_sum = lax.fori_loop(0, 4, multiply, jnp.zeros((16, 512), F32))
    scale_sum = jnp.zeros((1, 512), F32)
    for i in range(4):
        for k in range(4):
            scale_sum += jnp.sum(SL[i, k].astype(F32), axis=0, keepdims=True)
    weight = gain[:, pl.ds(pl.multiple_of(512 * x, 128), 512)]
    first_row = 516 * y - window_start(y)
    rows = lax.broadcasted_iota(jnp.int32, (16, 512), 0)
    for k in range(4):
        for i in range(4):
            start = first_row + 129 * k + 32 * i + jnp.where(x < i, 1, 0)
            zs[k, 32 * i : 32 * i + 32] = (rows_from(prod, start, 32) * weight).astype(BF16)
        extra = rows_from(prod, first_row + 129 * k + 32 * x + 32, 8)[0:1] * weight
        block = jnp.where(
            rows == 0, extra, jnp.where(rows == 1, cot_sum * weight, jnp.where(rows == 2, scale_sum, 0.0))
        )
        zs[k, 128:144] = block.astype(BF16)

    keep = pl.ds(pl.multiple_of(256 * c, 128), 256)
    give = pl.ds(pl.multiple_of(256 * (1 - c), 128), 256)
    across = remote(zs.at[:, :, give], cr, cs.at[0], crs.at[0], at(dc=1))
    send(across)
    across.wait_recv()
    for k in range(4):
        zb[k] = (zs[k, :, keep].astype(F32) + cr[k].astype(F32)).astype(BF16)

    for d in range(1, 8):
        send(remote(zb.at[lax.rem(z + d, 4)], zr.at[z], zss.at[d - 1], zrs.at[d - 1], at(dz=d)))
    zr[z] = zb[zl]
    for d in range(1, 8):
        ref = zr.at[wrap(z - d, 8)]
        remote(ref, ref, zss.at[d - 1], zrs.at[d - 1], at(dz=d)).wait_recv()
    group = zr[0].astype(F32)
    for k in range(1, 8):
        group += zr[k].astype(F32)

    for i in range(4):
        xs[i, 0:32] = group[32 * i : 32 * i + 32]
        xs[i, 32:40] = group[128:136]
    slot = 2 * x + c
    n = 0
    for dx in range(4):
        for dc in range(2):
            if dx or dc:
                send(remote(xs.at[wrap(x + dx, 4)], xr.at[slot], xss.at[n], xrs.at[n], at(dx=dx, dc=dc)))
                n += 1
    xr[slot] = xs[x]
    n = 0
    for dx in range(4):
        for dc in range(2):
            if dx or dc:
                ref = xr.at[2 * wrap(x - dx, 4) + wrap(c - dc, 2)]
                remote(ref, ref, xss.at[n], xrs.at[n], at(dx=dx, dc=dc)).wait_recv()
                n += 1

    last = jnp.where(f == 63, 1.0, 0.0).astype(F32)
    place = spot[0:1]
    pad[...] = jnp.zeros_like(pad)
    tg[...] = jnp.zeros_like(tg)
    for q in range(4):
        for h in range(2):
            for t in range(2):
                k = 4 * q + 2 * h + t
                pad[k : k + 1] = xr[2 * q + h, 33:34, 128 * t : 128 * t + 128] * last
                tg[TAIL_ROW + 240 + k : TAIL_ROW + 241 + k] = xr[2 * q + h, 34:35, 128 * t : 128 * t + 128] * last
    rolled = roll_by(pad[0:24], place, 1, range(7))
    lanes = lax.broadcasted_iota(jnp.int32, (24, 128), 1)
    pad[0:24] = jnp.where(lanes >= lax.rem(place, 128), rolled, pltpu.roll(rolled, 1, 0))
    tg[TAIL_ROW : TAIL_ROW + 256] += roll_by(pad[...], place, 0, range(7, 15))

    limit = PROJ - SHARD * f
    lanes = lax.broadcasted_iota(jnp.int32, (8, 128), 1)
    subs = lax.broadcasted_iota(jnp.int32, (8, 128), 0)

    def update(where, grad, inside):
        old = master[where]
        new_one = beta_one * one[where] + (1.0 - beta_one) * grad
        new_two = beta_two * two[where] + (1.0 - beta_two) * grad * grad
        first = new_one / (1.0 - beta_one**STEP)
        second = new_two / (1.0 - beta_two**STEP)
        decay = jnp.where(inside, decay_rate, 0.0) * old
        new = old - learn_rate * (first / (jnp.sqrt(second) + epsilon) + decay)
        master_out[where] = new
        one_out[where] = new_one
        two_out[where] = new_two
        teacher_out[where] = ema_rate * teacher[where] + (1.0 - ema_rate) * new

    for b in range(4):
        for m in range(4):
            q = wrap(x + m, 4)
            for t in range(4):
                base = 128 * b + 4 * m + t
                where = (pl.ds(base, 8, stride=16), slice(None))
                grad = xr[2 * q + t // 2, 8 * b : 8 * b + 8, 128 * (t % 2) : 128 * (t % 2) + 128]
                slots = 128 * base + 2048 * subs + lanes
                update(where, grad + tg[where], slots < limit)
    for t in range(4):
        where = (slice(512 + t, 513 + t), slice(None))
        grad = xr[2 * x + t // 2, 32:33, 128 * (t % 2) : 128 * (t % 2) + 128]
        update(where, grad * (1.0 - last) + tg[where], jnp.full((1, 128), 65536, jnp.int32) < limit)

    for copy in pending:
        copy.wait_send()


def step_kernel(tokens, cot, saved, gain, offsets, master, one, two, teacher):
    vmem = pl.BlockSpec(memory_space=pltpu.VMEM)
    anyspace = pl.BlockSpec(memory_space=pl.ANY)
    dma = pltpu.SemaphoreType.DMA
    flat = jax.ShapeDtypeStruct((FLAT, 128), F32)
    return pl.pallas_call(
        kernel,
        out_shape=[flat] * 4,
        in_specs=[vmem, vmem, anyspace, vmem, vmem, vmem, vmem, vmem, vmem],
        out_specs=[vmem] * 4,
        scratch_shapes=[
            pltpu.VMEM((4, 4, 128, WINDOW), BF16),
            pltpu.VMEM((4, 4, 128, 512), BF16),
            pltpu.VMEM((4, 4, 16, 512), BF16),
            pltpu.VMEM((4, 16, 512), BF16),
            pltpu.VMEM((WINDOW + 32, 512), F32),
            pltpu.VMEM((4, 144, 512), BF16),
            pltpu.VMEM((4, 144, 256), BF16),
            pltpu.VMEM((4, 144, 256), BF16),
            pltpu.VMEM((8, 144, 256), BF16),
            pltpu.VMEM((4, 40, 256), F32),
            pltpu.VMEM((8, 40, 256), F32),
            pltpu.VMEM((256, 128), F32),
            pltpu.VMEM((520, 128), F32),
            dma((2,)), dma((3,)), dma((3,)), dma((3,)), dma((3,)), dma((3,)), dma((3,)), dma((3,)), dma((3,)),
            dma((4, 6)), dma((4, 6)), dma((4, 6)), dma((4, 6)),
            dma((1,)), dma((1,)), dma((7,)), dma((7,)), dma((7,)), dma((7,)),
        ],
        compiler_params=pltpu.CompilerParams(
            collective_id=0, has_side_effects=True, vmem_limit_bytes=40 << 20
        ),
        name="step",
    )(jnp.full((8, 128), offsets[1] - PROJ, jnp.int32), gain, tokens, cot, saved, master, one, two, teacher)


def per_device(
    tokens, cotangent, saved_branch, layer_gain, offsets, master, moment_one, moment_two, teacher, teacher_tokens
):
    width_in = width_out = WIDTH
    start_proj, start_bias, start_scale = offsets[0], offsets[1], offsets[2]
    flat = [a.reshape(FLAT, 128) for a in (master, moment_one, moment_two, teacher)]
    outs = step_kernel(tokens, cotangent, saved_branch, layer_gain.reshape(1, WIDTH), offsets, *flat)
    master_new, moment_one_new, moment_two_new, teacher_new = [a.reshape(SHARD) for a in outs]
    teacher_low = teacher_new.astype(BF16)
    gathered = lax.all_gather(teacher_low, "fsdp", axis=0, tiled=True)
    proj_t = lax.dynamic_slice(gathered, (start_proj,), (width_in * width_out,)).reshape(width_in, width_out)
    bias_t = lax.dynamic_slice(gathered, (start_bias,), (width_out,)).astype(F32)
    scale_t = lax.dynamic_slice(gathered, (start_scale,), (width_out,)).astype(F32)
    product = jnp.dot(teacher_tokens, proj_t, preferred_element_type=F32)
    teacher_branch = (scale_t * (product + bias_t)).astype(BF16)
    return (master_new, moment_one_new, moment_two_new, teacher_new, teacher_branch)


def solution(mesh):
    rows = P(("fsdp", "dp"), None)
    return jax.shard_map(
        per_device,
        mesh=mesh,
        in_specs=(rows, rows, rows, P(), P(), P("fsdp"), P("fsdp"), P("fsdp"), P("fsdp"), rows),
        out_specs=(P("fsdp"), P("fsdp"), P("fsdp"), P("fsdp"), rows),
        check_vma=False,
    )
```

time: 1010 us -> 568 us (0.56)
  waiting for transfers between devices: 677 us -> 374 us
  local copies, waits for them, and re-layouts: 224 us -> 51.5 us
  Pallas kernels: 0 us -> 63.6 us
  blocking collectives: 10.5 us -> 0 us
    unnamed x3 -> x1, waiting for transfers between devices: 299 us -> 0.02 us
    dynamic_update_slice x3 -> x0, local copies, waits for them, and re-layouts: 144 us -> none  [the longest x1 142 us: per_device(): flat = lax.dynamic_update_slice(flat, grad_proj.reshape(-1), (start_proj,))]
    pallas_call x0 -> x1, Pallas kernels: none -> 63.6 us  [step_kernel(): pl.pallas_call(kernel, out_shape=[flat] * 4, in_specs=[vmem, vmem, anyspa...]
    dot_general x1 -> x0, local copies, waits for them, and re-layouts: 17.6 us -> none  [per_device(): lax.dot_general(tokens, weighted, (((0,), (0,)), ((), ())), preferred_ele...]
    all_gather x1 -> x0, blocking collectives: 10.5 us -> none  [per_device(): grad = lax.all_gather(summed_block, 'dp', axis=0, tiled=True)]
    unnamed x27 -> x25, local copies, waits for them, and re-layouts: 32.3 us -> 27.5 us
  transfers between devices with their start and end apart: 2 -> 1, of which waited for: 2 -> 1; matrix products, arithmetic and copies ran while one was open for 0% -> 0% of each run, Pallas kernels for 0% -> 0%
where the time goes in v1:
time: 568 us; the launch traced here: 566 us
  waiting for transfers between devices  374 us (66%)
  Pallas kernels  63.6 us (11%)
  local copies, waits for them, and re-layouts  51.5 us (9%)
  other arithmetic  51 us (9%)
  between operations  20.6 us (4%)
  matrix products  6.19 us (1%)
    all_gather x1, waiting for transfers between devices, per_device(): gathered = lax.all_gather(teacher_low, 'fsdp', axis=0, tiled=True)  373 us
    pallas_call x1, Pallas kernels, step_kernel(): pl.pallas_call(kernel, out_shape=[flat] * 4, in_specs=[vmem, vmem, anyspa...  63.6 us
    all_gather x1, other arithmetic, per_device(): gathered = lax.all_gather(teacher_low, 'fsdp', axis=0, tiled=True)  50.2 us
    unnamed x25, local copies, waits for them, and re-layouts  27.5 us
    reshape x1, local copies, waits for them, and re-layouts, per_device(): lax.dynamic_slice(gathered, (start_proj,), (width_in * width_out,))  13.3 us
  transfers between devices with their start and end apart: 1, of which 1 were waited for; matrix products, arithmetic and copies ran while one was open for 0% of the time, Pallas kernels for 0%

profile of v1, /device:TPU:2, one launch (start us, length us, event | category | flops | bytes accessed | tf_op | source)
XLA Modules:
  0.0 566.4 jit_solution(2859010794422117661)
XLA Ops:
  7.2 0.0 copy-start
  7.2 0.0 all-gather.3.cloned.1.call-start
  7.2 1.4 fusion.3
  9.2 0.0 copy-start.1
  9.3 1.0 copy-done.1
  10.3 0.0 copy-start.2
  10.3 1.0 copy-done.2
  11.3 0.0 copy-start.3
  11.3 1.0 copy-done.3
  12.4 0.0 copy-start.4
  12.4 0.9 copy-done.4
  13.3 0.0 copy-start.5
  13.3 0.9 copy-done.5
  14.3 0.0 copy-start.6
  14.3 0.9 copy-done.6
  15.2 0.0 copy-start.7
  15.2 0.9 copy-done.7
  16.2 0.0 copy-start.8
  16.2 0.7 copy-done.8
  16.9 63.6 %step.1 = (f32[516,128]{1,0:T(8,128)S(1)}, f32[516,128]{1,0:T(8,128)S(1)}, f32[516,128]{1,0:T(8,128)S(1)}, f32[516,128]{1,0:T(8,128)S(1)}) custom-call(s32[8,128]{1,0:T(8,128)S(1)} %broadcast_in_dim.2.spot, f32[1,2048]{1,0:T(1,128)S(1)} %bitcast.25, bf16[128,2048]{1,0:T(8,128)(2,1)S(1)} %copy-done.1, bf16[128,2048]{1,0:T(8,128)(2,1)S(1)} %copy-done.2, ...), custom_call_target="tpu_custom_call" | custom-call | tf_op jit(solution)/shard_map/step/pallas_call | solution.py:312
  80.5 0.8 reshape.52
  81.4 0.0 all-gather.3.cloned.1.call-update
  87.2 373.5 %all-gather.3.cloned.1.call-done = bf16[64,1,66048]{2,1,0:T(2,128)(2,1)} async-done(((bf16[1,1,66048]{2,1,0:T(2,128)(2,1)}), bf16[64,1,66048]{2,1,0:T(2,128)(2,1)}) %all-gather.3.cloned.1.call-update) | async-done | bytes 8454160 | tf_op jit(solution)/shard_map/all_gather | solution.py:351
  460.7 50.2 %reduce = bf16[64,66048]{1,0:T(8,128)(2,1)} reduce(bf16[64,1,66048]{2,1,0:T(2,128)(2,1)} %all-gather.3.cloned.1.call-done, bf16[]{:T(256)} %constant.11), dimensions={1}, to_apply=%all-gather.reduce_sub_computation | reduce | bytes 16908290 | tf_op jit(solution)/shard_map/all_gather | solution.py:351
  510.9 15.1 %reshape.53 = bf16[4227072]{0:T(1024)(128)(2,1)} reshape(bf16[64,66048]{1,0:T(8,128)(2,1)} %reduce) | data formatting | bytes 16908288
  526.0 9.3 %dynamic_slice.10 = bf16[4194304]{0:T(1024)(128)(2,1)} dynamic-slice(bf16[4227072]{0:T(1024)(128)(2,1)} %reshape.53, s32[]{:T(128)S(6)} %select_n.10), dynamic_slice_sizes={4194304} | dynamic-slice | bytes 16777220 | tf_op jit(solution)/shard_map/dynamic_slice | solution.py:352
  535.3 13.3 %reshape.51 = bf16[2048,2048]{1,0:T(8,128)(2,1)} reshape(bf16[4194304]{0:T(1024)(128)(2,1)} %dynamic_slice.10) | data formatting | bytes 16777216 | tf_op jit(solution)/shard_map/reshape | solution.py:352
  548.7 0.8 dynamic-slice_convert_fusion.1
  549.4 0.0 copy-done
  549.4 6.2 %fusion.2 = bf16[128,2048]{0,1:T(8,128)(2,1)S(1)} fusion(bf16[2048,2048]{1,0:T(8,128)(2,1)} %reshape.51, bf16[128,2048]{1,0:T(8,128)(2,1)S(1)} %copy-done, f32[2048]{0:T(1024)S(1)} %get-tuple-element.29, f32[2048]{0:T(1024)S(1)} %get-tuple-element.28), kind=kOutput, calls=%fused_computation.3 | convolution fusion | flops 1074528256 | bytes 9453568 | tf_op jit(solution)/shard_map/dot_general | solution.py:355
  555.6 1.0 copy.17
  556.6 0.7 copy.22
  557.4 0.7 copy.23
  558.1 0.7 copy.24
  558.8 0.7 copy.25
  (2 shorter events, 0.0 us)
Async XLA Ops:
  7.2 542.3 %copy-start = (bf16[128,2048]{1,0:T(8,128)(2,1)S(1)}, bf16[128,2048]{1,0:T(8,128)(2,1)}, u32[]{:S(2)}) copy-start(bf16[128,2048]{1,0:T(8,128)(2,1)} %param.19) | copy-start | bytes 1572868
  7.2 453.5 %all-gather.3.cloned.1.call-start = ((), (), s32[]{:S(2)}) async-start(), calls=%async_computation | async-start | bytes 17172480 | tf_op jit(solution)/shard_map/all_gather | solution.py:351
  9.2 1.0 copy-start.1
  10.3 1.0 copy-start.2
  11.3 1.0 copy-start.3
  12.4 1.0 copy-start.4
  13.3 1.0 copy-start.5
  14.3 1.0 copy-start.6
  15.2 1.0 copy-start.7
  16.2 0.7 copy-start.8
Sparse Core Ops, SparseCore 0:
  81.5 379.1 all-gather.2

commit v2 on v1

--- a/solution.py
+++ b/solution.py
@@ -69,10 +69,12 @@
 
 
 def kernel(
-    spot, gain, tokens, cot, saved, master, one, two, teacher,
-    master_out, one_out, two_out, teacher_out,
-    T, C, SL, SS, prod, zs, cr, zb, zr, xs, xr, pad, tg,
-    own_sem, a1s, a1r, b1s, b1r, s1s, s1r, s2s, s2r, a2s, a2r, b2s, b2r, cs, crs, zss, zrs, xss, xrs,
+    spot_hbm, gain_hbm, tokens, cot_hbm, saved_hbm, master_hbm, one_hbm, two_hbm, teacher_hbm, tt_hbm,
+    master_res, one_res, two_res, teacher_res, branch_res,
+    spot, gain, cot, saved, master, one, two, teacher, master_out, one_out, two_out, teacher_out,
+    T, C, SL, SS, prod, zs, cr, zb, zr, xs, xr, pad, tg, TT, S, TP, WF, WS, W, OUT,
+    in_sem, res_sem, own_sem, a1s, a1r, b1s, b1r, s1s, s1r, s2s, s2r, a2s, a2r, b2s, b2r, cs, crs, zss, zrs, xss, xrs,
+    ts, tr, w1s, w1r, w2s, w2r, w3s, w3r, os, orr,
 ):
     f = lax.axis_index("fsdp")
     p = lax.axis_index("dp")
@@ -90,7 +92,19 @@
         + [dict(dy=d) for d in (1, 2, 3)]
         + [dict(dz=d) for d in range(1, 8)]
         + [dict(dx=d, dc=1) for d in range(4)]
+        + [dict(dy=d, dc=1) for d in (1, 2, 3)]
     )
+    loads = [
+        pltpu.make_async_copy(src, dst, in_sem.at[k])
+        for k, (src, dst) in enumerate(
+            [
+                (cot_hbm, cot), (saved_hbm, saved), (tt_hbm, TT.at[jnp.where(c == 0, x, y), c]), (gain_hbm, gain),
+                (spot_hbm, spot), (master_hbm, master), (one_hbm, one), (two_hbm, two), (teacher_hbm, teacher),
+            ]
+        )
+    ]
+    for copy in loads:
+        copy.start()
     barrier = pltpu.get_barrier_semaphore()
     for partner in partners:
         pl.semaphore_signal(barrier, inc=1, device_id=at(**partner), device_id_type=MESH)
@@ -104,7 +118,7 @@
 
     mine = [
         pltpu.make_async_copy(tokens.at[:, pl.ds(window_start(y), WINDOW)], T.at[y, x], own_sem.at[0]),
-        pltpu.make_async_copy(cot.at[:, pl.ds(pl.multiple_of(512 * x, 128), 512)], C.at[y, x], own_sem.at[1]),
+        pltpu.make_async_copy(cot_hbm.at[:, pl.ds(pl.multiple_of(512 * x, 128), 512)], C.at[y, x], own_sem.at[1]),
     ]
     for copy in mine:
         copy.start()
@@ -112,7 +126,7 @@
         to_y = wrap(y + d, 4)
         send(remote(tokens.at[:, pl.ds(window_start(to_y), WINDOW)], T.at[y, x], a1s.at[d - 1], a1r.at[d - 1], at(dy=d)))
         to_x = wrap(x + d, 4)
-        send(remote(cot.at[:, pl.ds(pl.multiple_of(512 * to_x, 128), 512)], C.at[y, x], b1s.at[d - 1], b1r.at[d - 1], at(dx=d)))
+        send(remote(cot_hbm.at[:, pl.ds(pl.multiple_of(512 * to_x, 128), 512)], C.at[y, x], b1s.at[d - 1], b1r.at[d - 1], at(dx=d)))
     for copy in mine:
         copy.wait()
 
@@ -155,6 +169,66 @@
     spread_token(0)
     spread_cot(0)
 
+    a_own = jnp.where(c == 0, x, y)
+    a_twin = jnp.where(c == 0, y, x)
+    q = jnp.where(c == 0, lax.div(x, 2), 2 + lax.div(y, 2))
+
+    def ring(d):
+        return device(
+            jnp.where(c == 0, wrap(x + d, 4), x), jnp.where(c == 0, y, wrap(y + d, 4)), z, c
+        )
+
+    def cross(d):
+        return device(
+            jnp.where(c == 0, x, wrap(x + d, 4)), jnp.where(c == 0, wrap(y + d, 4), y), z, c
+        )
+
+    loads[2].wait()
+    send(remote(tt_hbm, TT.at[a_twin, c], ts.at[0, 6], tr.at[0, 6], at(dc=1)))
+
+    HALVES = [(low, 1), (high, 1), (high, -1), (low, -1)]
+
+    def spread_teacher(n, core):
+        for k, (half, d) in enumerate(HALVES):
+            ref = TT.at[a_own, core, half]
+            send(remote(ref, ref, ts.at[n, k], tr.at[n, k], ring(d)))
+
+    def teacher_wait(n, core, k):
+        half, d = [(low, -1), (high, -1), (high, 1), (low, 1), (low, -2), (high, 2)][k]
+        ref = TT.at[wrap(a_own + d, 4), core, half]
+        remote(ref, ref, ts.at[n, k], tr.at[n, k], ring(1)).wait_recv()
+        return ref
+
+    def relay_teacher(n, core):
+        for k, d in ((0, 1), (2, -1)):
+            ref = teacher_wait(n, core, k)
+            send(remote(ref, ref, ts.at[n, 4 + k // 2], tr.at[n, 4 + k // 2], ring(d)))
+
+    def one_hot(g, carry):
+        col = lax.broadcasted_iota(jnp.int32, (1, 384), 1)
+        place = lax.rem(col, 192)
+        i, r = lax.div(place, 48), lax.rem(place, 48)
+        source = 129 * (2 * g + lax.div(col, 192)) + 32 * i + r - jnp.minimum(256 * g, WIDTH - 384)
+        source = source + jnp.where(jnp.logical_and(r < 32, i > q), 1, 0)
+        source = jnp.where(jnp.logical_or(r < 32, jnp.logical_and(r == 32, i == q)), source, -1)
+        row = lax.broadcasted_iota(jnp.int32, (384, 384), 0)
+        S[g] = jnp.where(row == source, 1.0, 0.0).astype(BF16)
+        return carry
+
+    lax.fori_loop(0, 8, one_hot, 0)
+
+    def arrange(a):
+        def group(g, carry):
+            start = pl.multiple_of(jnp.minimum(256 * g, WIDTH - 384), 128)
+            for core in range(2):
+                part = jnp.dot(TT[a, core, :, pl.ds(start, 384)], S[g], preferred_element_type=F32)
+                TP[g, a, core] = part.astype(BF16)
+            return carry
+
+        lax.fori_loop(0, 8, group, 0)
+
+    loads[0].wait()
+    loads[1].wait()
     total = jnp.zeros((1, WIDTH), F32)
     for r in range(0, 128, 16):
         total += jnp.sum(cot[r : r + 16].astype(F32) * saved[r : r + 16].astype(F32), axis=0, keepdims=True)
@@ -182,6 +256,10 @@
     for d in (1, 2, 3):
         send(remote(SL.at[y], SL.at[y], s2s.at[d - 1], s2r.at[d - 1], at(dy=d)))
     relay(3)
+    spread_teacher(0, c)
+    ref = TT.at[a_own, 1 - c]
+    remote(ref, ref, ts.at[0, 6], tr.at[0, 6], at(dc=1)).wait_recv()
+    spread_teacher(1, 1 - c)
     for d in range(4):
         for k in (1, 3, 4, 5):
             token_wait(d, k)
@@ -190,6 +268,7 @@
         ref = SL.at[wrap(y - d, 4)]
         remote(ref, ref, s2s.at[d - 1], s2r.at[d - 1], at(dy=d)).wait_recv()
 
+    loads[3].wait()
     prod[...] = jnp.zeros_like(prod)
     ones = jnp.ones((16, 512), BF16)
 
@@ -221,6 +300,7 @@
     give = pl.ds(pl.multiple_of(256 * (1 - c), 128), 256)
     across = remote(zs.at[:, :, give], cr, cs.at[0], crs.at[0], at(dc=1))
     send(across)
+    relay_teacher(0, c)
     across.wait_recv()
     for k in range(4):
         zb[k] = (zs[k, :, keep].astype(F32) + cr[k].astype(F32)).astype(BF16)
@@ -228,6 +308,8 @@
     for d in range(1, 8):
         send(remote(zb.at[lax.rem(z + d, 4)], zr.at[z], zss.at[d - 1], zrs.at[d - 1], at(dz=d)))
     zr[z] = zb[zl]
+    relay_teacher(1, 1 - c)
+    arrange(a_own)
     for d in range(1, 8):
         ref = zr.at[wrap(z - d, 8)]
         remote(ref, ref, zss.at[d - 1], zrs.at[d - 1], at(dz=d)).wait_recv()
@@ -254,16 +336,17 @@
                 remote(ref, ref, xss.at[n], xrs.at[n], at(dx=dx, dc=dc)).wait_recv()
                 n += 1
 
+    for copy in loads[4:]:
+        copy.wait()
     last = jnp.where(f == 63, 1.0, 0.0).astype(F32)
     place = spot[0:1]
     pad[...] = jnp.zeros_like(pad)
     tg[...] = jnp.zeros_like(tg)
-    for q in range(4):
-        for h in range(2):
-            for t in range(2):
-                k = 4 * q + 2 * h + t
-                pad[k : k + 1] = xr[2 * q + h, 33:34, 128 * t : 128 * t + 128] * last
-                tg[TAIL_ROW + 240 + k : TAIL_ROW + 241 + k] = xr[2 * q + h, 34:35, 128 * t : 128 * t + 128] * last
+    for e in range(8):
+        for t in range(2):
+            k = 2 * e + t
+            pad[k : k + 1] = xr[e, 33:34, 128 * t : 128 * t + 128] * last
+            tg[TAIL_ROW + 240 + k : TAIL_ROW + 241 + k] = xr[e, 34:35, 128 * t : 128 * t + 128] * last
     rolled = roll_by(pad[0:24], place, 1, range(7))
     lanes = lax.broadcasted_iota(jnp.int32, (24, 128), 1)
     pad[0:24] = jnp.where(lanes >= lax.rem(place, 128), rolled, pltpu.roll(rolled, 1, 0))
@@ -284,37 +367,189 @@
         master_out[where] = new
         one_out[where] = new_one
         two_out[where] = new_two
-        teacher_out[where] = ema_rate * teacher[where] + (1.0 - ema_rate) * new
+        new_teacher = ema_rate * teacher[where] + (1.0 - ema_rate) * new
+        teacher_out[where] = new_teacher
+        return new_teacher
+
+    WF[:, 32:48] = jnp.zeros((8, 16, 256), F32)
 
     for b in range(4):
         for m in range(4):
-            q = wrap(x + m, 4)
+            quarter = wrap(x + m, 4)
             for t in range(4):
                 base = 128 * b + 4 * m + t
                 where = (pl.ds(base, 8, stride=16), slice(None))
-                grad = xr[2 * q + t // 2, 8 * b : 8 * b + 8, 128 * (t % 2) : 128 * (t % 2) + 128]
+                e, side = 2 * quarter + t // 2, slice(128 * (t % 2), 128 * (t % 2) + 128)
                 slots = 128 * base + 2048 * subs + lanes
-                update(where, grad + tg[where], slots < limit)
+                new = update(where, xr[e, 8 * b : 8 * b + 8, side] + tg[where], slots < limit)
+                WF[e, 8 * b : 8 * b + 8, side] = new
     for t in range(4):
         where = (slice(512 + t, 513 + t), slice(None))
-        grad = xr[2 * x + t // 2, 32:33, 128 * (t % 2) : 128 * (t % 2) + 128]
-        update(where, grad * (1.0 - last) + tg[where], jnp.full((1, 128), 65536, jnp.int32) < limit)
-
+        e, side = 2 * x + t // 2, slice(128 * (t % 2), 128 * (t % 2) + 128)
+        inside = jnp.full((1, 128), 65536, jnp.int32) < limit
+        WF[e, 32:33, side] = update(where, xr[e, 32:33, side] * (1.0 - last) + tg[where], inside)
+
+    tail = teacher_out[TAIL_ROW : TAIL_ROW + 256]
+    back = lax.rem(32768 - lax.div(place, 128) * 128, 32768)
+    moved = roll_by(tail, back, 0, range(7, 15))[0:24]
+    lane = lax.rem(place, 128)
+    rolled = roll_by(moved, lax.rem(128 - lane, 128), 1, range(7))
+    lanes = lax.broadcasted_iota(jnp.int32, (24, 128), 1)
+    bias = jnp.where(lanes < 128 - lane, rolled, pltpu.roll(rolled, 23, 0))
+    for e in range(8):
+        for t in range(2):
+            k, side = 2 * e + t, slice(128 * t, 128 * t + 128)
+            WF[e, 33:34, side] = bias[k : k + 1]
+            WF[e, 34:35, side] = tail[240 + k : 241 + k]
+    WS[...] = WF[...].astype(BF16)
+    results = [
+        pltpu.make_async_copy(src, dst, res_sem.at[k])
+        for k, (src, dst) in enumerate(
+            [(master_out, master_res), (one_out, one_res), (two_out, two_res), (teacher_out, teacher_res)]
+        )
+    ]
+
+    first = 4 * c
+    for d in (1, 2, 3):
+        send(remote(WS.at[first + wrap(a_own + d, 4)], W.at[y, zl, x], w1s.at[d - 1], w1r.at[d - 1], ring(d)))
+    W[y, zl, x] = WS[first + a_own]
+    for copy in results:
+        copy.start()
+
+    def columns(core):
+        def member(d):
+            return W.at[y, zl, wrap(x + d, 4)] if core == 0 else W.at[wrap(y + d, 4), zl, x]
+
+        def piece(layer, other, half=None):
+            span = pl.ds(0, 4) if half is None else pl.ds(2 * half, 2)
+            return W.at[other, layer, span] if core == 0 else W.at[span, layer, other]
+
+        here = y if core == 0 else x
+        started = []
+
+        def go(copy):
+            copy.start()
+            started.append(copy)
+
+        for d in (1, 2, 3):
+            ref = member(-d)
+            remote(ref, ref, w1s.at[d - 1], w1r.at[d - 1], ring(d)).wait_recv()
+        mine = piece(zl, here)
+        go(remote(mine, mine, w2s.at[0], w2r.at[0], at(dz=1)))
+        go(remote(mine, mine, w2s.at[1], w2r.at[1], at(dz=-1)))
+        ref = piece(zl, here, 0)
+        go(remote(ref, ref, w2s.at[2], w2r.at[2], at(dz=2)))
+        ref = piece(zl, here, 1)
+        go(remote(ref, ref, w2s.at[3], w2r.at[3], at(dz=-2)))
+
+        def spread(n, layer):
+            for k, (half, d) in enumerate([(0, 1), (1, 1), (1, -1), (0, -1)]):
+                ref = piece(layer, here, half)
+                go(remote(ref, ref, w3s.at[n, k], w3r.at[n, k], cross(d)))
+
+        def wait(n, layer, k):
+            half, d = [(0, -1), (1, -1), (1, 1), (0, 1), (0, -2), (1, 2)][k]
+            ref = piece(layer, wrap(here + d, 4), half)
+            remote(ref, ref, w3s.at[n, k], w3r.at[n, k], cross(1)).wait_recv()
+            return ref
+
+        def pass_on(n, layer):
+            for k, d in ((0, 1), (2, -1)):
+                ref = wait(n, layer, k)
+                go(remote(ref, ref, w3s.at[n, 4 + k // 2], w3r.at[n, 4 + k // 2], cross(d)))
+
+        layers = [zl, wrap(zl - 1, 4), wrap(zl + 1, 4), wrap(zl + 2, 4)]
+        spread(0, layers[0])
+        arrange(wrap(a_own + 2, 4))
+        for n, k in ((1, 0), (2, 1)):
+            ref = piece(layers[n], here)
+            remote(ref, ref, w2s.at[k], w2r.at[k], at(dz=1)).wait_recv()
+            spread(n, layers[n])
+        for k in (2, 3):
+            ref = piece(layers[3], here, k - 2)
+            remote(ref, ref, w2s.at[k], w2r.at[k], at(dz=1)).wait_recv()
+        spread(3, layers[3])
+        for n in range(4):
+            pass_on(n, layers[n])
+        for n in range(4):
+            for k in (1, 3, 4, 5):
+                wait(n, layers[n], k)
+        for copy in started:
+            copy.wait_send()
+
+    for n, core in ((0, c), (1, 1 - c)):
+        for k in (1, 3, 4, 5):
+            teacher_wait(n, core, k)
+    arrange(wrap(a_own + 1, 4))
+    arrange(wrap(a_own + 3, 4))
+
+    @pl.when(c == 0)
+    def _():
+        columns(0)
+
+    @pl.when(c == 1)
+    def _():
+        columns(1)
+
+    bias_t = W[3, 3, 3, 32:48].astype(F32)[1:2]
+    scale_t = W[3, 3, 3, 32:48].astype(F32)[2:3]
+
+    def finish(a, carry):
+        total = jnp.zeros((256, 256), F32)
+        for g in range(8):
+            left = TP[g, a].reshape(256, 384)
+            right = W[g // 2, 2 * (g % 2) : 2 * (g % 2) + 2].reshape(384, 256)
+            total += jnp.dot(left, right, preferred_element_type=F32)
+        OUT[a] = (scale_t * (total + bias_t)).astype(BF16).reshape(2, 128, 256)
+        return carry
+
+    lax.fori_loop(0, 4, finish, 0)
+    e_own = first + a_own
+    out_cols = branch_res.at[:, pl.ds(pl.multiple_of(256 * e_own, 128), 256)]
+    n = 0
+    for d in range(4):
+        for dc in range(2):
+            if d or dc:
+                a = wrap(a_own + d, 4)
+                core = wrap(c + dc, 2)
+                to = device(jnp.where(c == 0, a, x), jnp.where(c == 0, y, a), z, core)
+                send(remote(OUT.at[a, core], out_cols, os.at[n], orr.at[e_own], to))
+                n += 1
+    stay = pltpu.make_async_copy(OUT.at[a_own, c], out_cols, own_sem.at[2])
+    stay.start()
+    for e in range(8):
+
+        @pl.when(e != e_own)
+        def _():
+            ref = branch_res.at[:, pl.ds(256 * e, 256)]
+            remote(ref, ref, os.at[0], orr.at[e], at(dc=1)).wait_recv()
+
+    stay.wait()
+    for copy in results:
+        copy.wait()
     for copy in pending:
         copy.wait_send()
 
 
-def step_kernel(tokens, cot, saved, gain, offsets, master, one, two, teacher):
-    vmem = pl.BlockSpec(memory_space=pltpu.VMEM)
+def per_device(
+    tokens, cotangent, saved_branch, layer_gain, offsets, master, moment_one, moment_two, teacher, teacher_tokens
+):
     anyspace = pl.BlockSpec(memory_space=pl.ANY)
     dma = pltpu.SemaphoreType.DMA
     flat = jax.ShapeDtypeStruct((FLAT, 128), F32)
-    return pl.pallas_call(
+    shard = pltpu.VMEM((FLAT, 128), F32)
+    spot = jnp.full((8, 128), offsets[1] - PROJ, jnp.int32)
+    outs = pl.pallas_call(
         kernel,
-        out_shape=[flat] * 4,
-        in_specs=[vmem, vmem, anyspace, vmem, vmem, vmem, vmem, vmem, vmem],
-        out_specs=[vmem] * 4,
+        out_shape=[flat] * 4 + [jax.ShapeDtypeStruct((128, WIDTH), BF16)],
+        in_specs=[anyspace] * 10,
+        out_specs=[anyspace] * 5,
         scratch_shapes=[
+            pltpu.VMEM((8, 128), jnp.int32),
+            pltpu.VMEM((1, WIDTH), F32),
+            pltpu.VMEM((128, WIDTH), BF16),
+            pltpu.VMEM((128, WIDTH), BF16),
+            shard, shard, shard, shard, shard, shard, shard, shard,
             pltpu.VMEM((4, 4, 128, WINDOW), BF16),
             pltpu.VMEM((4, 4, 128, 512), BF16),
             pltpu.VMEM((4, 4, 16, 512), BF16),
@@ -328,33 +563,27 @@
             pltpu.VMEM((8, 40, 256), F32),
             pltpu.VMEM((256, 128), F32),
             pltpu.VMEM((520, 128), F32),
-            dma((2,)), dma((3,)), dma((3,)), dma((3,)), dma((3,)), dma((3,)), dma((3,)), dma((3,)), dma((3,)),
+            pltpu.VMEM((4, 2, 128, WIDTH), BF16),
+            pltpu.VMEM((8, 384, 384), BF16),
+            pltpu.VMEM((8, 4, 2, 128, 384), BF16),
+            pltpu.VMEM((8, 48, 256), F32),
+            pltpu.VMEM((8, 48, 256), BF16),
+            pltpu.VMEM((4, 4, 4, 48, 256), BF16),
+            pltpu.VMEM((4, 2, 128, 256), BF16),
+            dma((9,)), dma((4,)), dma((3,)),
+            dma((3,)), dma((3,)), dma((3,)), dma((3,)), dma((3,)), dma((3,)), dma((3,)), dma((3,)),
             dma((4, 6)), dma((4, 6)), dma((4, 6)), dma((4, 6)),
             dma((1,)), dma((1,)), dma((7,)), dma((7,)), dma((7,)), dma((7,)),
+            dma((2, 7)), dma((2, 7)), dma((3,)), dma((3,)), dma((4,)), dma((4,)), dma((4, 6)), dma((4, 6)),
+            dma((7,)), dma((8,)),
         ],
-        compiler_params=pltpu.CompilerParams(
-            collective_id=0, has_side_effects=True, vmem_limit_bytes=40 << 20
-        ),
+        compiler_params=pltpu.CompilerParams(collective_id=0, has_side_effects=True, vmem_limit_bytes=56 << 20),
         name="step",
-    )(jnp.full((8, 128), offsets[1] - PROJ, jnp.int32), gain, tokens, cot, saved, master, one, two, teacher)
-
-
-def per_device(
-    tokens, cotangent, saved_branch, layer_gain, offsets, master, moment_one, moment_two, teacher, teacher_tokens
-):
-    width_in = width_out = WIDTH
-    start_proj, start_bias, start_scale = offsets[0], offsets[1], offsets[2]
-    flat = [a.reshape(FLAT, 128) for a in (master, moment_one, moment_two, teacher)]
-    outs = step_kernel(tokens, cotangent, saved_branch, layer_gain.reshape(1, WIDTH), offsets, *flat)
-    master_new, moment_one_new, moment_two_new, teacher_new = [a.reshape(SHARD) for a in outs]
-    teacher_low = teacher_new.astype(BF16)
-    gathered = lax.all_gather(teacher_low, "fsdp", axis=0, tiled=True)
-    proj_t = lax.dynamic_slice(gathered, (start_proj,), (width_in * width_out,)).reshape(width_in, width_out)
-    bias_t = lax.dynamic_slice(gathered, (start_bias,), (width_out,)).astype(F32)
-    scale_t = lax.dynamic_slice(gathered, (start_scale,), (width_out,)).astype(F32)
-    product = jnp.dot(teacher_tokens, proj_t, preferred_element_type=F32)
-    teacher_branch = (scale_t * (product + bias_t)).astype(BF16)
-    return (master_new, moment_one_new, moment_two_new, teacher_new, teacher_branch)
+    )(
+        spot, layer_gain.reshape(1, WIDTH), tokens, cotangent, saved_branch,
+        *[a.reshape(FLAT, 128) for a in (master, moment_one, moment_two, teacher)], teacher_tokens,
+    )
+    return tuple(a.reshape(SHARD) for a in outs[:4]) + (outs[4],)
 
 
 def solution(mesh):

time: 568 us -> 107 us (0.19)
  the two profiles are of different devices: /device:TPU:2 before, /device:TPU:1 now
where the time goes in v2:
time: 107 us
  Pallas kernels  98.4 us (92%)
  local copies, waits for them, and re-layouts  6.83 us (6%)
  between operations  1.31 us (1%)
    pallas_call x1, Pallas kernels, per_device(): pl.pallas_call(kernel, out_shape=[flat] * 4 + [jax.ShapeDtypeStruct((128,...  98.4 us
    unnamed x15, local copies, waits for them, and re-layouts  5.66 us

profile of v2, /device:TPU:1, one launch (start us, length us, event | category | flops | bytes accessed | tf_op | source)
XLA Modules:
  0.0 106.6 jit_solution(15043877730559024481)
XLA Ops:
  0.6 0.0 copy-start.4
  0.6 0.6 copy-done.4
  1.3 0.6 slice.3
  2.5 0.6 broadcast_in_dim.3.spot_hbm
  3.1 98.4 %step.1 = (f32[516,128]{1,0:T(8,128)}, f32[516,128]{1,0:T(8,128)}, f32[516,128]{1,0:T(8,128)}, f32[516,128]{1,0:T(8,128)}, bf16[128,2048]{1,0:T(8,128)(2,1)}) custom-call(s32[8,128]{1,0:T(8,128)} %broadcast_in_dim.3.spot_hbm, f32[1,2048]{1,0:T(1,128)} %bitcast.18, bf16[128,2048]{1,0:T(8,128)(2,1)} %tokens.1, bf16[128,2048]{1,0:T(8,128)(2,1)} %cot_hbm.1, ...), custom_call_target="tpu_custom_call" | custom-call | tf_op jit(solution)/shard_map/step/pallas_call | solution.py:542
  101.5 0.0 copy-start.3
  101.6 1.7 %copy.20 = f32[66048]{0:T(1024)} copy(f32[66048]{0:T(1024)} %bitcast.17) | data formatting | bytes 528384
  103.3 0.0 copy-done.3
  103.3 0.0 copy-start.2
  103.3 0.0 copy-start.1
  103.3 0.7 copy.21
  104.0 0.3 copy-done.2
  104.3 0.0 copy-start
  104.3 0.7 copy.22
  105.0 0.0 copy-done.1
  105.0 0.7 copy.23
  105.8 0.0 copy-done
  105.8 0.8 copy.24
Async XLA Ops:
  0.6 0.7 copy-start.4
  101.5 1.7 %copy-start.3 = (f32[516,128]{1,0:T(8,128)S(1)}, f32[516,128]{1,0:T(8,128)}, u32[]{:S(2)}) copy-start(f32[516,128]{1,0:T(8,128)} %get-tuple-element.11) | copy-start | bytes 792580
  103.3 1.0 copy-start.2
  103.3 1.8 %copy-start.1 = (f32[516,128]{1,0:T(8,128)S(1)}, f32[516,128]{1,0:T(8,128)}, u32[]{:S(2)}) copy-start(f32[516,128]{1,0:T(8,128)} %get-tuple-element.13) | copy-start | bytes 792580
  104.3 1.5 %copy-start = (bf16[128,2048]{1,0:T(8,128)(2,1)S(1)}, bf16[128,2048]{1,0:T(8,128)(2,1)}, u32[]{:S(2)}) copy-start(bf16[128,2048]{1,0:T(8,128)(2,1)} %get-tuple-element.24) | copy-start | bytes 1572868

commit v3 on v1

v3 whole, which is shorter than its diff:
```python
import jax
import jax.numpy as jnp
from jax import lax
from jax.experimental import pallas as pl
from jax.experimental.pallas import tpu as pltpu
from jax.sharding import PartitionSpec as P

MESH = pl.DeviceIdType.MESH
F32 = jnp.float32
BF16 = jnp.bfloat16

STEP = 1000
beta_one = 0.9
beta_two = 0.999
learn_rate = 0.001
decay_rate = 0.04
ema_rate = 0.994
epsilon = 1e-08

WIDTH = 2048
PROJ = WIDTH * WIDTH
SHARD = 66048
FLAT = SHARD // 128
TAIL = 260
GROUP = 144


def wrap(value, size):
    return lax.rem(value + size, size)


def device(x, y, z, c):
    return (y * 16 + lax.rem(z, 4) * 4 + x, lax.div(z, 4) * 2 + c)


def remote(src, dst, send, recv, to):
    return pltpu.make_async_remote_copy(
        src_ref=src, dst_ref=dst, send_sem=send, recv_sem=recv, device_id=to, device_id_type=MESH
    )


def roll_by(value, amount, axis, bits):
    for bit in bits:
        on = jnp.broadcast_to(lax.rem(lax.div(amount, 2**bit), 2) == 1, value.shape)
        value = jnp.where(on, pltpu.roll(value, 2 ** (bit - bits[0]), axis), value)
    return value


def iota(shape, axis):
    return lax.broadcasted_iota(jnp.int32, shape, axis)


def kernel(
    offsets, gain_hbm, tokens_hbm, cot_hbm, saved_hbm, master_hbm, one_hbm, two_hbm, teacher_hbm, tt_hbm,
    master_res, one_res, two_res, teacher_res, branch_res,
    gain, tok, cot, saved, master, one, two, teacher, mix, master_out, one_out, two_out, teacher_out,
    TW, T, C, SL, SS, prod, zs, cr, zb, zr, PS, PR, xs, xr, pad, tg, TT, S, TP, TE, W, acc, OUT,
    in_sem, res_sem, own_sem, a1s, a1r, b1s, b1r, s1s, s1r, s2s, s2r, a2s, a2r, b2s, b2r, cs, crs, zss, zrs,
    ps, prs, xss, xrs, ts, tr, us, ur, w2s, w2r, w3s, w3r, os, orr,
):
    f = lax.axis_index("fsdp")
    p = lax.axis_index("dp")
    x = lax.rem(f, 4)
    zl = lax.rem(lax.div(f, 4), 4)
    y = lax.div(f, 16)
    c = lax.rem(p, 2)
    z = lax.div(p, 2) * 4 + zl

    def at(dx=0, dy=0, dz=0, dc=0):
        return device(wrap(x + dx, 4), wrap(y + dy, 4), wrap(z + dz, 8), wrap(c + dc, 2))

    partners = (
        [dict(dx=d) for d in (1, 2, 3)]
        + [dict(dy=d) for d in (1, 2, 3)]
        + [dict(dz=d) for d in range(1, 8)]
        + [dict(dx=d, dc=1) for d in range(4)]
    )
    loads = [
        pltpu.make_async_copy(src, dst, in_sem.at[k])
        for k, (src, dst) in enumerate(
            [
                (tokens_hbm, tok), (cot_hbm, cot), (saved_hbm, saved), (tt_hbm, TT.at[x, c]), (gain_hbm, gain),
                (master_hbm, master), (one_hbm, one), (two_hbm, two), (teacher_hbm, teacher),
            ]
        )
    ]
    for copy in loads:
        copy.start()
    barrier = pltpu.get_barrier_semaphore()
    for partner in partners:
        pl.semaphore_signal(barrier, inc=1, device_id=at(**partner), device_id_type=MESH)
    pl.semaphore_wait(barrier, len(partners))

    pending = []

    def send(copy):
        copy.start()
        pending.append(copy)

    def ring(view, halves, to, sends, recvs):
        def spread(n):
            for k, (half, d) in enumerate([(0, 1), (1, 1), (1, -1), (0, -1)]):
                ref = view(n, 0, halves[half])
                send(remote(ref, ref, sends.at[n, k], recvs.at[n, k], to(d)))

        def wait(n, k):
            half, d = [(0, -1), (1, -1), (1, 1), (0, 1), (0, -2), (1, 2)][k]
            ref = view(n, d, halves[half])
            remote(ref, ref, sends.at[n, k], recvs.at[n, k], to(1)).wait_recv()
            return ref

        def relay(n):
            for k, d in ((0, 1), (2, -1)):
                ref = wait(n, k)
                send(remote(ref, ref, sends.at[n, 4 + k // 2], recvs.at[n, 4 + k // 2], to(d)))

        return spread, wait, relay

    halves = [pl.ds(0, 64), pl.ds(64, 64)]
    along_x = lambda d: at(dx=d)
    along_y = lambda d: at(dy=d)
    spread_t, wait_t, relay_t = ring(
        lambda n, d, half: T.at[wrap(y - n, 4), wrap(x + d, 4), half], halves, along_x, a2s, a2r
    )
    spread_c, wait_c, relay_c = ring(
        lambda n, d, half: C.at[wrap(y + d, 4), wrap(x - n, 4), half], halves, along_y, b2s, b2r
    )
    spread_h, wait_h, relay_h = ring(
        lambda n, d, half: TT.at[wrap(x + d, 4), c, half], halves, along_x, ts, tr
    )

    def quarter(i):
        return cot_hbm.at[:, pl.ds(pl.multiple_of(512 * i, 128), 512)]

    mine = pltpu.make_async_copy(quarter(x), C.at[y, x], own_sem.at[0])
    mine.start()
    for d in (1, 2, 3):
        send(remote(quarter(wrap(x + d, 4)), C.at[y, x], b1s.at[d - 1], b1r.at[d - 1], at(dx=d)))
    loads[0].wait()
    for i in range(4):
        end = min(512 * i + 640, WIDTH)
        window = tok[:, 512 * i : end].astype(F32)
        if i:
            window = pltpu.roll(window, end - 512 * i - 4 * i, 1)[:, :512]
        else:
            window = window[:, :512]
        if i == 3:
            window = jnp.where(iota((128, 512), 1) < 500, window, 0.0)
        TW[i] = window.astype(BF16)
    for d in (1, 2, 3):
        send(remote(TW.at[wrap(y + d, 4)], T.at[y, x], a1s.at[d - 1], a1r.at[d - 1], at(dy=d)))
    T[y, x] = TW[y]
    spread_t(0)
    mine.wait()
    spread_c(0)
    loads[3].wait()
    send(remote(TT.at[x, c], TT.at[x, c], us.at[0], ur.at[0], at(dc=1)))
    for d in (1, 2, 3):
        ref = T.at[wrap(y - d, 4), x]
        remote(ref, ref, a1s.at[d - 1], a1r.at[d - 1], at(dy=d)).wait_recv()
        spread_t(d)
        ref = C.at[y, wrap(x - d, 4)]
        remote(ref, ref, b1s.at[d - 1], b1r.at[d - 1], at(dx=d)).wait_recv()
        spread_c(d)
        relay_t(d - 1)
        relay_c(d - 1)

    loads[1].wait()
    loads[2].wait()
    total = jnp.zeros((1, WIDTH), F32)
    for r in range(0, 128, 16):
        total += jnp.sum(cot[r : r + 16].astype(F32) * saved[r : r + 16].astype(F32), axis=0, keepdims=True)
    top = total.astype(BF16).astype(F32)
    lane = iota((128, 128), 1)
    left = jnp.zeros((128, 128), F32)
    for i in range(3):
        tile = tok[:, 512 * (i + 1) : 512 * (i + 1) + 128].astype(F32)
        left = jnp.where(jnp.logical_and(lane >= 4 * i, lane < 4 * i + 4), tile, left)
    rows = iota((16, 512), 0)
    for i in range(4):
        side = slice(512 * i, 512 * i + 512)
        part = lax.dot_general(
            left.astype(BF16), cot[:, side], (((0,), (0,)), ((), ())), preferred_element_type=F32
        )[:16]
        part = jnp.where(rows == 12, top[:, side], jnp.where(rows == 13, total[:, side] - top[:, side], part))
        SS[i] = part.astype(BF16)
    for d in (1, 2, 3):
        send(remote(SS.at[wrap(x + d, 4)], SL.at[y, x], s1s.at[d - 1], s1r.at[d - 1], at(dx=d)))
    SL[y, x] = SS[x]

    for copy in loads[4:]:
        copy.wait()
    limit = PROJ - SHARD * f
    spots = 128 * iota((FLAT, 128), 0) + iota((FLAT, 128), 1)
    keep = jnp.where(spots < limit, 1.0 - learn_rate * decay_rate, 1.0)
    mix[...] = ema_rate * teacher[...] + (1.0 - ema_rate) * keep * master[...]
    place = jnp.full((1, 128), offsets[1] - PROJ, jnp.int32)
    row_back = lax.rem(32768 - lax.div(place, 128) * 128, 32768)
    lane_at = lax.rem(place, 128)
    lane_back = lax.rem(128 - lane_at, 128)
    lanes24 = iota((24, 128), 1)
    low_core = c == 0
    for k, source in enumerate((mix, one, two)):
        for b in range(4):
            for m in range(4):
                for t in range(2):
                    low = source[pl.ds(128 * b + 4 * m + t, 8, stride=16), :]
                    high = source[pl.ds(128 * b + 4 * m + 2 + t, 8, stride=16), :]
                    PS[wrap(x + m, 4), k, 8 * b : 8 * b + 8, 128 * t : 128 * t + 128] = jnp.where(low_core, low, high)
        tail = source[TAIL : TAIL + 256]
        moved = roll_by(tail, row_back, 0, range(7, 15))[0:24]
        rolled = roll_by(moved, lane_back, 1, range(7))
        bias = jnp.where(lanes24 < 128 - lane_at, rolled, pltpu.roll(rolled, 23, 0))
        for m in range(4):
            for t in range(2):
                side = slice(128 * t, 128 * t + 128)
                n = 4 * m + t
                PS[m, k, 32:33, side] = jnp.where(low_core, source[512 + t : 513 + t], source[514 + t : 515 + t])
                PS[m, k, 33:34, side] = jnp.where(low_core, bias[n : n + 1], bias[n + 2 : n + 3])
                PS[m, k, 34:35, side] = jnp.where(low_core, tail[240 + n : 241 + n], tail[242 + n : 243 + n])
                PS[m, k, 35:40, side] = jnp.zeros((5, 128), F32)

    for d in (1, 2, 3):
        ref = SL.at[y, wrap(x - d, 4)]
        remote(ref, ref, s1s.at[d - 1], s1r.at[d - 1], at(dx=d)).wait_recv()
    for d in (1, 2, 3):
        send(remote(SL.at[y], SL.at[y], s2s.at[d - 1], s2r.at[d - 1], at(dy=d)))
    relay_t(3)
    relay_c(3)
    for d in (1, 2, 3):
        send(remote(PS.at[wrap(x + d, 4)], PR.at[x], ps.at[d - 1], prs.at[d - 1], at(dx=d)))
    PR[x] = PS[x]
    spread_h(0)

    def one_hot(g, carry):
        col = iota((1, 384), 1)
        i = lax.div(lax.rem(col, 128), 32)
        source = 258 * g + lax.div(col, 128) * 129 + lax.rem(col, 128) + jnp.where(i > x, 1, 0)
        slot = lax.rem(col, 128) - 32 * lax.rem(g, 4)
        extra = 258 * g + 32 * x + 32 + jnp.where(slot == 0, 0, 129)
        extra = jnp.where(jnp.logical_or(slot == 0, slot == 16), extra, -1)
        source = jnp.where(col < 256, source, extra) - jnp.minimum(256 * g, WIDTH - 384)
        S[g] = jnp.where(iota((384, 384), 0) == source, 1.0, 0.0).astype(BF16)
        return carry

    lax.fori_loop(0, 8, one_hot, 0)

    def arrange(a):
        def group(g, extra):
            start = pl.multiple_of(jnp.minimum(256 * g, WIDTH - 384), 128)
            block = TT[a, :, :, pl.ds(start, 384)].reshape(256, 384)
            part = jnp.dot(block, S[g], preferred_element_type=F32)
            TP[g, a] = part[:, :256].astype(BF16)
            return extra + part[:, 256:]

        for h in range(2):
            extra = lax.fori_loop(4 * h, 4 * h + 4, group, jnp.zeros((256, 128), F32))
            TE[a, :, 128 * h : 128 * h + 128] = extra.astype(BF16)

    for n in range(4):
        for k in (1, 3, 4, 5):
            wait_t(n, k)
            wait_c(n, k)
    for d in (1, 2, 3):
        ref = SL.at[wrap(y - d, 4)]
        remote(ref, ref, s2s.at[d - 1], s2r.at[d - 1], at(dy=d)).wait_recv()

    prod[0:512] = jnp.zeros((512, 512), F32)
    ones = jnp.ones((16, 512), BF16)

    def multiply(k, sums):
        right = C[k].reshape(512, 512)
        prod[0:512] += lax.dot_general(
            T[k].reshape(512, 512), right, (((0,), (0,)), ((), ())), preferred_element_type=F32
        )
        return sums + jnp.dot(ones, right, preferred_element_type=F32)

    cot_sum = lax.fori_loop(0, 4, multiply, jnp.zeros((16, 512), F32))
    small = jnp.zeros((16, 512), F32)
    for i in range(4):
        for k in range(4):
            small += SL[i, k].astype(F32)
    rest = jnp.where(y == 0, small, jnp.where(y == 1, pltpu.roll(small, 12, 0), pltpu.roll(small, 8, 0)))
    prod[512:528] = jnp.where(rows < jnp.where(y < 3, 4, 0), rest, 0.0)
    weight = gain[:, pl.ds(pl.multiple_of(512 * x, 128), 512)]
    for k in range(4):
        for i in range(4):
            start = 129 * k + 32 * i
            part = prod[start : start + 32]
            if i:
                part = jnp.where(x < i, prod[start + 1 : start + 33], part)
            zs[k, 32 * i : 32 * i + 32] = (part * weight).astype(BF16)
        extra = prod[129 * k + 32 : 129 * k + 33]
        for i in range(1, 4):
            extra = jnp.where(x == i, prod[129 * k + 32 * i + 32 : 129 * k + 32 * i + 33], extra)
        block = jnp.where(rows == 1, cot_sum * weight, jnp.where(rows == 2, small[12:13] + small[13:14], 0.0))
        zs[k, 128:144] = jnp.where(rows == 0, extra * weight, block).astype(BF16)

    keep_half = pl.ds(pl.multiple_of(256 * c, 128), 256)
    give_half = pl.ds(pl.multiple_of(256 * (1 - c), 128), 256)
    across = remote(zs.at[:, :, give_half], cr, cs.at[0], crs.at[0], at(dc=1))
    send(across)
    relay_h(0)
    across.wait_recv()
    for k in range(4):
        zb[k] = (zs[k, :, keep_half].astype(F32) + cr[k].astype(F32)).astype(BF16)

    for d in range(1, 8):
        send(remote(zb.at[lax.rem(z + d, 4)], zr.at[z], zss.at[d - 1], zrs.at[d - 1], at(dz=d)))
    zr[z] = zb[zl]
    ref = TT.at[x, 1 - c]
    remote(ref, ref, us.at[0], ur.at[0], at(dc=1)).wait_recv()
    arrange(x)
    for d in (1, 2, 3):
        ref = PR.at[wrap(x - d, 4)]
        remote(ref, ref, ps.at[d - 1], prs.at[d - 1], at(dx=d)).wait_recv()
    for d in range(1, 8):
        ref = zr.at[wrap(z - d, 8)]
        remote(ref, ref, zss.at[d - 1], zrs.at[d - 1], at(dz=d)).wait_recv()
    group = zr[0].astype(F32)
    for k in range(1, 8):
        group += zr[k].astype(F32)

    def low_teacher(grad, mixed, old_one, old_two):
        new_one = beta_one * old_one + (1.0 - beta_one) * grad
        new_two = beta_two * old_two + (1.0 - beta_two) * grad * grad
        first = new_one / (1.0 - beta_one**STEP)
        second = new_two / (1.0 - beta_two**STEP)
        return mixed - ((1.0 - ema_rate) * learn_rate) * (first / (jnp.sqrt(second) + epsilon))

    for i in range(4):
        span = slice(32 * i, 32 * i + 32)
        W[y, zl, span] = low_teacher(group[span], *[PR[i, k, 0:32] for k in range(3)]).astype(BF16)
    first_row = iota((8, 256), 0) == 0
    extras = [jnp.where(first_row, PR[x, k, 32:40], PR[3, k, 32:40]) for k in range(3)]
    block = low_teacher(group[128:136], *extras)
    block = jnp.where(iota((8, 256), 0) < 3, block, 0.0)
    W[y, zl, 128:144] = jnp.concatenate([block, jnp.zeros((8, 256), F32)], axis=0).astype(BF16)

    parts = [pl.ds(0, 80), pl.ds(80, 64)]
    layers = [zl, wrap(zl - 1, 4), wrap(zl + 1, 4), wrap(zl + 2, 4)]
    spread_w, wait_w, relay_w = ring(
        lambda n, d, half: W.at[wrap(y + d, 4), layers[n], half], parts, along_y, w3s, w3r
    )
    for k, (ref, d) in enumerate(
        [(W.at[y, zl], 1), (W.at[y, zl], -1), (W.at[y, zl, parts[0]], 2), (W.at[y, zl, parts[1]], -2)]
    ):
        send(remote(ref, ref, w2s.at[k], w2r.at[k], at(dz=d)))
    spread_w(0)

    for i in range(4):
        xs[i, 0:32] = group[32 * i : 32 * i + 32]
        xs[i, 32:40] = group[128:136]
    slot = 2 * x + c
    others = [(dx, dc) for dx in range(4) for dc in range(2) if dx or dc]
    for n, (dx, dc) in enumerate(others):
        send(remote(xs.at[wrap(x + dx, 4)], xr.at[slot], xss.at[n], xrs.at[n], at(dx=dx, dc=dc)))
    xr[slot] = xs[x]

    def share(n, d, arrivals):
        for k in arrivals:
            wait_h(0, k)
        ref = TT.at[wrap(x + d, 4), c]
        send(remote(ref, ref, us.at[n], ur.at[n], at(dc=1)))

    def shared(n, d):
        ref = TT.at[wrap(x + d, 4), 1 - c]
        remote(ref, ref, us.at[n], ur.at[n], at(dc=1)).wait_recv()

    share(1, -1, (1,))
    share(2, 1, (3,))
    for n, k in ((1, 0), (2, 1)):
        ref = W.at[y, layers[n]]
        remote(ref, ref, w2s.at[k], w2r.at[k], at(dz=1)).wait_recv()
        spread_w(n)
    for k in (2, 3):
        ref = W.at[y, layers[3], parts[k - 2]]
        remote(ref, ref, w2s.at[k], w2r.at[k], at(dz=1)).wait_recv()
    spread_w(3)
    relay_w(0)
    shared(1, -1)
    arrange(wrap(x - 1, 4))
    share(3, 2, (4, 5))
    relay_w(1)
    shared(2, 1)
    arrange(wrap(x + 1, 4))
    relay_w(2)

    def accumulate(i, a):
        total = jnp.zeros((256, 256), F32)
        for h in range(2):
            right = W[i, 2 * h : 2 * h + 2, 0:128].reshape(256, 256)
            total += jnp.dot(TP[2 * i + h, a], right, preferred_element_type=F32)
        return total

    relay_w(3)
    shared(3, 2)
    arrange(wrap(x + 2, 4))

    for n, (dx, dc) in enumerate(others):
        ref = xr.at[2 * wrap(x - dx, 4) + wrap(c - dc, 2)]
        remote(ref, ref, xss.at[n], xrs.at[n], at(dx=dx, dc=dc)).wait_recv()
    last = jnp.where(f == 63, 1.0, 0.0).astype(F32)
    pad[...] = jnp.zeros_like(pad)
    tg[...] = jnp.zeros_like(tg)
    for e in range(8):
        for t in range(2):
            n = 2 * e + t
            pad[n : n + 1] = xr[e, 33:34, 128 * t : 128 * t + 128] * last
            tg[TAIL + 240 + n : TAIL + 241 + n] = xr[e, 34:35, 128 * t : 128 * t + 128] * last
    rolled = roll_by(pad[0:24], place, 1, range(7))
    pad[0:24] = jnp.where(lanes24 >= lane_at, rolled, pltpu.roll(rolled, 1, 0))
    tg[TAIL : TAIL + 256] += roll_by(pad[...], place, 0, range(7, 15))
    lanes = iota((8, 128), 1)
    subs = iota((8, 128), 0)

    def update(where, grad, inside):
        old = master[where]
        new_one = beta_one * one[where] + (1.0 - beta_one) * grad
        new_two = beta_two * two[where] + (1.0 - beta_two) * grad * grad
        first = new_one / (1.0 - beta_one**STEP)
        second = new_two / (1.0 - beta_two**STEP)
        decay = jnp.where(inside, decay_rate, 0.0) * old
        new = old - learn_rate * (first / (jnp.sqrt(second) + epsilon) + decay)
        master_out[where] = new
        one_out[where] = new_one
        two_out[where] = new_two
        teacher_out[where] = ema_rate * teacher[where] + (1.0 - ema_rate) * new

    for b in range(4):
        for m in range(4):
            for t in range(4):
                base = 128 * b + 4 * m + t
                where = (pl.ds(base, 8, stride=16), slice(None))
                e, side = 2 * wrap(x + m, 4) + t // 2, slice(128 * (t % 2), 128 * (t % 2) + 128)
                slots = 128 * base + 2048 * subs + lanes
                update(where, xr[e, 8 * b : 8 * b + 8, side] + tg[where], slots < limit)
    for t in range(4):
        where = (slice(512 + t, 513 + t), slice(None))
        e, side = 2 * x + t // 2, slice(128 * (t % 2), 128 * (t % 2) + 128)
        inside = jnp.full((1, 128), 65536, jnp.int32) < limit
        update(where, xr[e, 32:33, side] * (1.0 - last) + tg[where], inside)
    results = [
        pltpu.make_async_copy(src, dst, res_sem.at[k])
        for k, (src, dst) in enumerate(
            [(master_out, master_res), (one_out, one_res), (two_out, two_res), (teacher_out, teacher_res)]
        )
    ]
    for copy in results:
        copy.start()

    def begin(a, carry):
        acc[a] = accumulate(y, a)
        return carry

    lax.fori_loop(0, 4, begin, 0)
    for d, arrivals in ((-1, (1,)), (1, (3,)), (2, (4, 5))):
        for n in range(4):
            for k in arrivals:
                wait_w(n, k)
        if d != 2:

            def more(a, carry):
                acc[a] += accumulate(wrap(y + d, 4), a)
                return carry

            lax.fori_loop(0, 4, more, 0)

    bias_t = W[3, 3, 128:144].astype(F32)[1:2]
    scale_t = W[3, 3, 128:144].astype(F32)[2:3]
    ends = W[:, :, 128:144].reshape(256, 256)
    out_cols = branch_res.at[:, pl.ds(pl.multiple_of(256 * slot, 128), 256)]
    n = 0
    for d in (2, 1, 3, 0):
        a = wrap(x + d, 4)
        total = acc[a] + accumulate(wrap(y + 2, 4), a) + jnp.dot(TE[a], ends, preferred_element_type=F32)
        OUT[a] = (scale_t * (total + bias_t)).astype(BF16).reshape(2, 128, 256)
        for dc in range(2):
            core = wrap(c + dc, 2)
            if d or dc:
                send(remote(OUT.at[a, core], out_cols, os.at[n], orr.at[slot], at(dx=d, dc=dc)))
                n += 1
    stay = pltpu.make_async_copy(OUT.at[x, c], out_cols, own_sem.at[1])
    stay.start()
    for n, (dx, dc) in enumerate(others):
        e = 2 * wrap(x - dx, 4) + wrap(c - dc, 2)
        ref = branch_res.at[:, pl.ds(pl.multiple_of(256 * e, 128), 256)]
        remote(ref, ref, os.at[n], orr.at[e], at(dc=1)).wait_recv()
    stay.wait()
    for copy in results:
        copy.wait()
    for copy in pending:
        copy.wait_send()


def copy_kernel(*refs):
    sems = refs[10]
    copies = [pltpu.make_async_copy(refs[k], refs[5 + k], sems.at[k]) for k in range(5)]
    for copy in copies:
        copy.start()
    for copy in copies:
        copy.wait()


def per_device(
    tokens, cotangent, saved_branch, layer_gain, offsets, master, moment_one, moment_two, teacher, teacher_tokens
):
    anyspace = pl.BlockSpec(memory_space=pl.ANY)
    dma = pltpu.SemaphoreType.DMA
    flat = jax.ShapeDtypeStruct((FLAT, 128), F32)
    shard = pltpu.VMEM((FLAT, 128), F32)
    rows = pltpu.VMEM((128, WIDTH), BF16)
    results = [flat] * 4 + [jax.ShapeDtypeStruct((128, WIDTH), BF16)]
    outs = pl.pallas_call(
        kernel,
        out_shape=results,
        in_specs=[pl.BlockSpec(memory_space=pltpu.SMEM)] + [anyspace] * 9,
        out_specs=[anyspace] * 5,
        scratch_shapes=[
            pltpu.VMEM((1, WIDTH), F32),
            rows, rows, rows,
            shard, shard, shard, shard, shard, shard, shard, shard, shard,
            pltpu.VMEM((4, 128, 512), BF16),
            pltpu.VMEM((4, 4, 128, 512), BF16),
            pltpu.VMEM((4, 4, 128, 512), BF16),
            pltpu.VMEM((4, 4, 16, 512), BF16),
            pltpu.VMEM((4, 16, 512), BF16),
            pltpu.VMEM((528, 512), F32),
            pltpu.VMEM((4, GROUP, 512), BF16),
            pltpu.VMEM((4, GROUP, 256), BF16),
            pltpu.VMEM((4, GROUP, 256), BF16),
            pltpu.VMEM((8, GROUP, 256), BF16),
            pltpu.VMEM((4, 3, 40, 256), F32),
            pltpu.VMEM((4, 3, 40, 256), F32),
            pltpu.VMEM((4, 40, 256), F32),
            pltpu.VMEM((8, 40, 256), F32),
            pltpu.VMEM((256, 128), F32),
            pltpu.VMEM((520, 128), F32),
            pltpu.VMEM((4, 2, 128, WIDTH), BF16),
            pltpu.VMEM((8, 384, 384), BF16),
            pltpu.VMEM((8, 4, 256, 256), BF16),
            pltpu.VMEM((4, 256, 256), BF16),
            pltpu.VMEM((4, 4, GROUP, 256), BF16),
            pltpu.VMEM((4, 256, 256), F32),
            pltpu.VMEM((4, 2, 128, 256), BF16),
            dma((9,)), dma((4,)), dma((2,)),
            dma((3,)), dma((3,)), dma((3,)), dma((3,)), dma((3,)), dma((3,)), dma((3,)), dma((3,)),
            dma((4, 6)), dma((4, 6)), dma((4, 6)), dma((4, 6)),
            dma((1,)), dma((1,)), dma((7,)), dma((7,)),
            dma((3,)), dma((3,)), dma((7,)), dma((7,)),
            dma((1, 6)), dma((1, 6)), dma((4,)), dma((4,)), dma((4,)), dma((4,)), dma((4, 6)), dma((4, 6)),
            dma((7,)), dma((8,)),
        ],
        compiler_params=pltpu.CompilerParams(collective_id=0, has_side_effects=True, vmem_limit_bytes=56 << 20),
        name="step",
    )(
        offsets, layer_gain.reshape(1, WIDTH), tokens, cotangent, saved_branch,
        *[a.reshape(FLAT, 128) for a in (master, moment_one, moment_two, teacher)], teacher_tokens,
    )
    outs = pl.pallas_call(
        copy_kernel,
        out_shape=results,
        in_specs=[anyspace] * 5,
        out_specs=[anyspace] * 5,
        scratch_shapes=[dma((5,))],
        name="place",
    )(*outs)
    return tuple(a.reshape(SHARD) for a in outs[:4]) + (outs[4],)


def solution(mesh):
    rows = P(("fsdp", "dp"), None)
    return jax.shard_map(
        per_device,
        mesh=mesh,
        in_specs=(rows, rows, rows, P(), P(), P("fsdp"), P("fsdp"), P("fsdp"), P("fsdp"), rows),
        out_specs=(P("fsdp"), P("fsdp"), P("fsdp"), P("fsdp"), rows),
        check_vma=False,
    )
```

time: 568 us -> 139 us (0.24)
  the two profiles are of different devices: /device:TPU:2 before, /device:TPU:1 now
where the time goes in v3:
time: 139 us
  Pallas kernels  138 us (99%)
    pallas_call x1, Pallas kernels, per_device(): pl.pallas_call(kernel, out_shape=results, in_specs=[pl.BlockSpec(memory_s...  89.3 us
    pallas_call x1, Pallas kernels, per_device(): pl.pallas_call(copy_kernel, out_shape=results, in_specs=[anyspace] * 5, o...  49 us

profile of v3, /device:TPU:1, one launch (start us, length us, event | category | flops | bytes accessed | tf_op | source)
XLA Modules:
  0.0 138.9 jit_solution(12909676526794426801)
XLA Ops:
  0.6 89.3 %step.1 = (f32[516,128]{1,0:T(8,128)}, f32[516,128]{1,0:T(8,128)}, f32[516,128]{1,0:T(8,128)}, f32[516,128]{1,0:T(8,128)}, bf16[128,2048]{1,0:T(8,128)(2,1)}) custom-call(s32[3]{0:T(128)} %offsets.1, f32[1,2048]{1,0:T(1,128)} %bitcast.13, bf16[128,2048]{1,0:T(8,128)(2,1)} %tokens_hbm.1, bf16[128,2048]{1,0:T(8,128)(2,1)} %cot_hbm.1, ...), custom_call_target="tpu_custom_call" | custom-call | tf_op jit(solution)/shard_map/step/pallas_call | solution.py:514
  89.9 49.0 %place.1 = (f32[516,128]{1,0:T(8,128)}, f32[516,128]{1,0:T(8,128)}, f32[516,128]{1,0:T(8,128)}, f32[516,128]{1,0:T(8,128)}, bf16[128,2048]{1,0:T(8,128)(2,1)}) custom-call(f32[516,128]{1,0:T(8,128)} %get-tuple-element.15.refs_0_, f32[516,128]{1,0:T(8,128)} %get-tuple-element.16.refs_1_, f32[516,128]{1,0:T(8,128)} %get-tuple-element.17.refs_2_, ...), custom_call_target="tpu_custom_call" | custom-call | tf_op jit(solution)/shard_map/place/pallas_call | solution.py:560

commit v4 on v3

--- a/solution.py
+++ b/solution.py
@@ -54,7 +54,7 @@
     offsets, gain_hbm, tokens_hbm, cot_hbm, saved_hbm, master_hbm, one_hbm, two_hbm, teacher_hbm, tt_hbm,
     master_res, one_res, two_res, teacher_res, branch_res,
     gain, tok, cot, saved, master, one, two, teacher, mix, master_out, one_out, two_out, teacher_out,
-    TW, T, C, SL, SS, prod, zs, cr, zb, zr, PS, PR, xs, xr, pad, tg, TT, S, TP, TE, W, acc, OUT,
+    TW, T, C, SX, SL, SS, prod, zs, cr, zb, zr, PS, PR, xs, xr, pad, tg, TT, S, TP, TE, W, acc, OUT,
     in_sem, res_sem, own_sem, a1s, a1r, b1s, b1r, s1s, s1r, s2s, s2r, a2s, a2r, b2s, b2r, cs, crs, zss, zrs,
     ps, prs, xss, xrs, ts, tr, us, ur, w2s, w2r, w3s, w3r, os, orr,
 ):
@@ -155,16 +155,6 @@
     spread_c(0)
     loads[3].wait()
     send(remote(TT.at[x, c], TT.at[x, c], us.at[0], ur.at[0], at(dc=1)))
-    for d in (1, 2, 3):
-        ref = T.at[wrap(y - d, 4), x]
-        remote(ref, ref, a1s.at[d - 1], a1r.at[d - 1], at(dy=d)).wait_recv()
-        spread_t(d)
-        ref = C.at[y, wrap(x - d, 4)]
-        remote(ref, ref, b1s.at[d - 1], b1r.at[d - 1], at(dx=d)).wait_recv()
-        spread_c(d)
-        relay_t(d - 1)
-        relay_c(d - 1)
-
     loads[1].wait()
     loads[2].wait()
     total = jnp.zeros((1, WIDTH), F32)
@@ -185,8 +175,30 @@
         part = jnp.where(rows == 12, top[:, side], jnp.where(rows == 13, total[:, side] - top[:, side], part))
         SS[i] = part.astype(BF16)
     for d in (1, 2, 3):
-        send(remote(SS.at[wrap(x + d, 4)], SL.at[y, x], s1s.at[d - 1], s1r.at[d - 1], at(dx=d)))
-    SL[y, x] = SS[x]
+        send(remote(SS.at[wrap(x + d, 4)], SX.at[x], s1s.at[d - 1], s1r.at[d - 1], at(dx=d)))
+    SX[x] = SS[x]
+
+    for d, before in ((1, 0), (3, 1), (2, 3)):
+        ref = T.at[wrap(y - d, 4), x]
+        remote(ref, ref, a1s.at[d - 1], a1r.at[d - 1], at(dy=d)).wait_recv()
+        spread_t(d)
+        ref = C.at[y, wrap(x - d, 4)]
+        remote(ref, ref, b1s.at[d - 1], b1r.at[d - 1], at(dx=d)).wait_recv()
+        spread_c(d)
+        relay_t(before)
+        relay_c(before)
+
+    for d in (1, 2, 3):
+        ref = SX.at[wrap(x - d, 4)]
+        remote(ref, ref, s1s.at[d - 1], s1r.at[d - 1], at(dx=d)).wait_recv()
+    small = jnp.zeros((16, 512), F32)
+    for i in range(4):
+        small += SX[i].astype(F32)
+    total = small[12:13] + small[13:14]
+    top = total.astype(BF16).astype(F32)
+    SL[y] = jnp.where(rows == 12, top, jnp.where(rows == 13, total - top, small)).astype(BF16)
+    for d in (1, 2, 3):
+        send(remote(SL.at[y], SL.at[y], s2s.at[d - 1], s2r.at[d - 1], at(dy=d)))
 
     for copy in loads[4:]:
         copy.wait()
@@ -220,13 +232,8 @@
                 PS[m, k, 34:35, side] = jnp.where(low_core, tail[240 + n : 241 + n], tail[242 + n : 243 + n])
                 PS[m, k, 35:40, side] = jnp.zeros((5, 128), F32)
 
-    for d in (1, 2, 3):
-        ref = SL.at[y, wrap(x - d, 4)]
-        remote(ref, ref, s1s.at[d - 1], s1r.at[d - 1], at(dx=d)).wait_recv()
-    for d in (1, 2, 3):
-        send(remote(SL.at[y], SL.at[y], s2s.at[d - 1], s2r.at[d - 1], at(dy=d)))
-    relay_t(3)
-    relay_c(3)
+    relay_t(2)
+    relay_c(2)
     for d in (1, 2, 3):
         send(remote(PS.at[wrap(x + d, 4)], PR.at[x], ps.at[d - 1], prs.at[d - 1], at(dx=d)))
     PR[x] = PS[x]
@@ -257,29 +264,30 @@
             extra = lax.fori_loop(4 * h, 4 * h + 4, group, jnp.zeros((256, 128), F32))
             TE[a, :, 128 * h : 128 * h + 128] = extra.astype(BF16)
 
-    for n in range(4):
+    ones = jnp.ones((16, 512), BF16)
+    cot_sum = jnp.zeros((16, 512), F32)
+    for n, arrivals in ((0, ()), (1, (1,)), (3, (3,)), (2, (4, 5))):
         for k in (1, 3, 4, 5):
             wait_t(n, k)
-            wait_c(n, k)
+        for k in arrivals:
+            for i in range(4):
+                wait_c(i, k)
+        row = wrap(y - n, 4)
+        right = C[row].reshape(512, 512)
+        part = lax.dot_general(
+            T[row].reshape(512, 512), right, (((0,), (0,)), ((), ())), preferred_element_type=F32
+        )
+        if n:
+            prod[0:512] += part
+        else:
+            prod[0:512] = part
+        cot_sum += jnp.dot(ones, right, preferred_element_type=F32)
+
+    small = SL[y].astype(F32)
     for d in (1, 2, 3):
         ref = SL.at[wrap(y - d, 4)]
         remote(ref, ref, s2s.at[d - 1], s2r.at[d - 1], at(dy=d)).wait_recv()
-
-    prod[0:512] = jnp.zeros((512, 512), F32)
-    ones = jnp.ones((16, 512), BF16)
-
-    def multiply(k, sums):
-        right = C[k].reshape(512, 512)
-        prod[0:512] += lax.dot_general(
-            T[k].reshape(512, 512), right, (((0,), (0,)), ((), ())), preferred_element_type=F32
-        )
-        return sums + jnp.dot(ones, right, preferred_element_type=F32)
-
-    cot_sum = lax.fori_loop(0, 4, multiply, jnp.zeros((16, 512), F32))
-    small = jnp.zeros((16, 512), F32)
-    for i in range(4):
-        for k in range(4):
-            small += SL[i, k].astype(F32)
+        small += SL[wrap(y - d, 4)].astype(F32)
     rest = jnp.where(y == 0, small, jnp.where(y == 1, pltpu.roll(small, 12, 0), pltpu.roll(small, 8, 0)))
     prod[512:528] = jnp.where(rows < jnp.where(y < 3, 4, 0), rest, 0.0)
     weight = gain[:, pl.ds(pl.multiple_of(512 * x, 128), 512)]
@@ -310,7 +318,23 @@
     zr[z] = zb[zl]
     ref = TT.at[x, 1 - c]
     remote(ref, ref, us.at[0], ur.at[0], at(dc=1)).wait_recv()
+    def share(n, d, arrivals):
+        for k in arrivals:
+            wait_h(0, k)
+        ref = TT.at[wrap(x + d, 4), c]
+        send(remote(ref, ref, us.at[n], ur.at[n], at(dc=1)))
+
+    def shared(n, d):
+        ref = TT.at[wrap(x + d, 4), 1 - c]
+        remote(ref, ref, us.at[n], ur.at[n], at(dc=1)).wait_recv()
+
     arrange(x)
+    share(1, -1, (1,))
+    share(2, 1, (3,))
+    shared(1, -1)
+    arrange(wrap(x - 1, 4))
+    shared(2, 1)
+    arrange(wrap(x + 1, 4))
     for d in (1, 2, 3):
         ref = PR.at[wrap(x - d, 4)]
         remote(ref, ref, ps.at[d - 1], prs.at[d - 1], at(dx=d)).wait_recv()
@@ -357,18 +381,6 @@
         send(remote(xs.at[wrap(x + dx, 4)], xr.at[slot], xss.at[n], xrs.at[n], at(dx=dx, dc=dc)))
     xr[slot] = xs[x]
 
-    def share(n, d, arrivals):
-        for k in arrivals:
-            wait_h(0, k)
-        ref = TT.at[wrap(x + d, 4), c]
-        send(remote(ref, ref, us.at[n], ur.at[n], at(dc=1)))
-
-    def shared(n, d):
-        ref = TT.at[wrap(x + d, 4), 1 - c]
-        remote(ref, ref, us.at[n], ur.at[n], at(dc=1)).wait_recv()
-
-    share(1, -1, (1,))
-    share(2, 1, (3,))
     for n, k in ((1, 0), (2, 1)):
         ref = W.at[y, layers[n]]
         remote(ref, ref, w2s.at[k], w2r.at[k], at(dz=1)).wait_recv()
@@ -378,12 +390,8 @@
         remote(ref, ref, w2s.at[k], w2r.at[k], at(dz=1)).wait_recv()
     spread_w(3)
     relay_w(0)
-    shared(1, -1)
-    arrange(wrap(x - 1, 4))
     share(3, 2, (4, 5))
     relay_w(1)
-    shared(2, 1)
-    arrange(wrap(x + 1, 4))
     relay_w(2)
 
     def accumulate(i, a):
@@ -494,11 +502,15 @@
 
 
 def copy_kernel(*refs):
-    sems = refs[10]
-    copies = [pltpu.make_async_copy(refs[k], refs[5 + k], sems.at[k]) for k in range(5)]
-    for copy in copies:
+    sems = refs[15]
+    loads = [pltpu.make_async_copy(refs[k], refs[10 + k], sems.at[k]) for k in range(5)]
+    stores = [pltpu.make_async_copy(refs[10 + k], refs[5 + k], sems.at[5 + k]) for k in range(5)]
+    for copy in loads:
         copy.start()
-    for copy in copies:
+    for load, store in zip(loads, stores):
+        load.wait()
+        store.start()
+    for copy in stores:
         copy.wait()
 
 
@@ -523,7 +535,8 @@
             pltpu.VMEM((4, 128, 512), BF16),
             pltpu.VMEM((4, 4, 128, 512), BF16),
             pltpu.VMEM((4, 4, 128, 512), BF16),
-            pltpu.VMEM((4, 4, 16, 512), BF16),
+            pltpu.VMEM((4, 16, 512), BF16),
+            pltpu.VMEM((4, 16, 512), BF16),
             pltpu.VMEM((4, 16, 512), BF16),
             pltpu.VMEM((528, 512), F32),
             pltpu.VMEM((4, GROUP, 512), BF16),
@@ -562,7 +575,7 @@
         out_shape=results,
         in_specs=[anyspace] * 5,
         out_specs=[anyspace] * 5,
-        scratch_shapes=[dma((5,))],
+        scratch_shapes=[shard, shard, shard, shard, rows, dma((10,))],
         name="place",
     )(*outs)
     return tuple(a.reshape(SHARD) for a in outs[:4]) + (outs[4],)

time: 139 us -> 91.2 us (0.66)
  Pallas kernels: 138 us -> 90.4 us
    pallas_call x1, Pallas kernels: 49 us -> 2.24 us  [per_device(): pl.pallas_call(copy_kernel, out_shape=results, in_specs=[anyspace] * 5, o...]
where the time goes in v4:
time: 91.2 us; the launch traced here: 91.1 us
  Pallas kernels  90.4 us (99%)
    pallas_call x1, Pallas kernels, per_device(): pl.pallas_call(kernel, out_shape=results, in_specs=[pl.BlockSpec(memory_s...  88.2 us
    pallas_call x1, Pallas kernels, per_device(): pl.pallas_call(copy_kernel, out_shape=results, in_specs=[anyspace] * 5, o...  2.24 us

profile of v4, /device:TPU:1, one launch (start us, length us, event | category | flops | bytes accessed | tf_op | source)
XLA Modules:
  0.0 91.1 jit_solution(8043324440827932973)
XLA Ops:
  0.6 88.2 %step.1 = (f32[516,128]{1,0:T(8,128)}, f32[516,128]{1,0:T(8,128)}, f32[516,128]{1,0:T(8,128)}, f32[516,128]{1,0:T(8,128)}, bf16[128,2048]{1,0:T(8,128)(2,1)}) custom-call(s32[3]{0:T(128)} %offsets.1, f32[1,2048]{1,0:T(1,128)} %bitcast.13, bf16[128,2048]{1,0:T(8,128)(2,1)} %tokens_hbm.1, bf16[128,2048]{1,0:T(8,128)(2,1)} %cot_hbm.1, ...), custom_call_target="tpu_custom_call" | custom-call | tf_op jit(solution)/shard_map/step/pallas_call | solution.py:526
  88.8 2.2 %place.1 = (f32[516,128]{1,0:T(8,128)}, f32[516,128]{1,0:T(8,128)}, f32[516,128]{1,0:T(8,128)}, f32[516,128]{1,0:T(8,128)}, bf16[128,2048]{1,0:T(8,128)(2,1)}) custom-call(f32[516,128]{1,0:T(8,128)} %get-tuple-element.15.refs_0_, f32[516,128]{1,0:T(8,128)} %get-tuple-element.16.refs_1_, f32[516,128]{1,0:T(8,128)} %get-tuple-element.17.refs_2_, ...), custom_call_target="tpu_custom_call" | custom-call | tf_op jit(solution)/shard_map/place/pallas_call | solution.py:573

commit v5 on v4

--- a/solution.py
+++ b/solution.py
@@ -54,9 +54,9 @@
     offsets, gain_hbm, tokens_hbm, cot_hbm, saved_hbm, master_hbm, one_hbm, two_hbm, teacher_hbm, tt_hbm,
     master_res, one_res, two_res, teacher_res, branch_res,
     gain, tok, cot, saved, master, one, two, teacher, mix, master_out, one_out, two_out, teacher_out,
-    TW, T, C, SX, SL, SS, prod, zs, cr, zb, zr, PS, PR, xs, xr, pad, tg, TT, S, TP, TE, W, acc, OUT,
+    TW, T, C, SX, SL, SS, prod, zs, cr, zb, zr, PS, PR, both, xs, xr, pad, tg, TT, S, TP, TE, W, acc, OUT,
     in_sem, res_sem, own_sem, a1s, a1r, b1s, b1r, s1s, s1r, s2s, s2r, a2s, a2r, b2s, b2r, cs, crs, zss, zrs,
-    ps, prs, xss, xrs, ts, tr, us, ur, w2s, w2r, w3s, w3r, os, orr,
+    ps, prs, xss, xrs, ts, tr, us, ur, w2s, w2r, w3s, w3r, hs, hr, os, orr,
 ):
     f = lax.axis_index("fsdp")
     p = lax.axis_index("dp")
@@ -75,6 +75,7 @@
         + [dict(dz=d) for d in range(1, 8)]
         + [dict(dx=d, dc=1) for d in range(4)]
     )
+    h = lax.div(z, 4)
     loads = [
         pltpu.make_async_copy(src, dst, in_sem.at[k])
         for k, (src, dst) in enumerate(
@@ -211,26 +212,23 @@
     lane_at = lax.rem(place, 128)
     lane_back = lax.rem(128 - lane_at, 128)
     lanes24 = iota((24, 128), 1)
-    low_core = c == 0
+    mine_of = lambda four: jnp.where(
+        c == 0, jnp.where(h == 0, four[0], four[1]), jnp.where(h == 0, four[2], four[3])
+    )
     for k, source in enumerate((mix, one, two)):
         for b in range(4):
             for m in range(4):
-                for t in range(2):
-                    low = source[pl.ds(128 * b + 4 * m + t, 8, stride=16), :]
-                    high = source[pl.ds(128 * b + 4 * m + 2 + t, 8, stride=16), :]
-                    PS[wrap(x + m, 4), k, 8 * b : 8 * b + 8, 128 * t : 128 * t + 128] = jnp.where(low_core, low, high)
+                four = [source[pl.ds(128 * b + 4 * m + t, 8, stride=16), :] for t in range(4)]
+                PS[wrap(x + m, 4), k, 8 * b : 8 * b + 8] = mine_of(four)
         tail = source[TAIL : TAIL + 256]
         moved = roll_by(tail, row_back, 0, range(7, 15))[0:24]
         rolled = roll_by(moved, lane_back, 1, range(7))
         bias = jnp.where(lanes24 < 128 - lane_at, rolled, pltpu.roll(rolled, 23, 0))
         for m in range(4):
-            for t in range(2):
-                side = slice(128 * t, 128 * t + 128)
-                n = 4 * m + t
-                PS[m, k, 32:33, side] = jnp.where(low_core, source[512 + t : 513 + t], source[514 + t : 515 + t])
-                PS[m, k, 33:34, side] = jnp.where(low_core, bias[n : n + 1], bias[n + 2 : n + 3])
-                PS[m, k, 34:35, side] = jnp.where(low_core, tail[240 + n : 241 + n], tail[242 + n : 243 + n])
-                PS[m, k, 35:40, side] = jnp.zeros((5, 128), F32)
+            PS[m, k, 32:33] = mine_of([source[512 + t : 513 + t] for t in range(4)])
+            PS[m, k, 33:34] = mine_of([bias[4 * m + t : 4 * m + t + 1] for t in range(4)])
+            PS[m, k, 34:35] = mine_of([tail[240 + 4 * m + t : 241 + 4 * m + t] for t in range(4)])
+            PS[m, k, 35:40] = jnp.zeros((5, 128), F32)
 
     relay_t(2)
     relay_c(2)
@@ -290,6 +288,8 @@
         small += SL[wrap(y - d, 4)].astype(F32)
     rest = jnp.where(y == 0, small, jnp.where(y == 1, pltpu.roll(small, 12, 0), pltpu.roll(small, 8, 0)))
     prod[512:528] = jnp.where(rows < jnp.where(y < 3, 4, 0), rest, 0.0)
+    keep_half = pl.ds(pl.multiple_of(256 * c, 128), 256)
+    give_half = pl.ds(pl.multiple_of(256 * (1 - c), 128), 256)
     weight = gain[:, pl.ds(pl.multiple_of(512 * x, 128), 512)]
     for k in range(4):
         for i in range(4):
@@ -303,21 +303,21 @@
             extra = jnp.where(x == i, prod[129 * k + 32 * i + 32 : 129 * k + 32 * i + 33], extra)
         block = jnp.where(rows == 1, cot_sum * weight, jnp.where(rows == 2, small[12:13] + small[13:14], 0.0))
         zs[k, 128:144] = jnp.where(rows == 0, extra * weight, block).astype(BF16)
-
-    keep_half = pl.ds(pl.multiple_of(256 * c, 128), 256)
-    give_half = pl.ds(pl.multiple_of(256 * (1 - c), 128), 256)
-    across = remote(zs.at[:, :, give_half], cr, cs.at[0], crs.at[0], at(dc=1))
-    send(across)
+        send(remote(zs.at[k, :, give_half], cr.at[k], cs.at[k], crs.at[k], at(dc=1)))
     relay_h(0)
-    across.wait_recv()
-    for k in range(4):
-        zb[k] = (zs[k, :, keep_half].astype(F32) + cr[k].astype(F32)).astype(BF16)
-
-    for d in range(1, 8):
-        send(remote(zb.at[lax.rem(z + d, 4)], zr.at[z], zss.at[d - 1], zrs.at[d - 1], at(dz=d)))
-    zr[z] = zb[zl]
-    ref = TT.at[x, 1 - c]
-    remote(ref, ref, us.at[0], ur.at[0], at(dc=1)).wait_recv()
+
+    for j in range(4):
+        k = wrap(zl + j, 4)
+        remote(zs.at[k, :, give_half], cr.at[k], cs.at[k], crs.at[k], at(dc=1)).wait_recv()
+        chip = (zs[k, :, keep_half].astype(F32) + cr[k].astype(F32)).astype(BF16)
+        zb[k] = chip[:, :128]
+        zb[4 + k] = chip[:, 128:]
+        for d in (j, j + 4):
+            if d:
+                to_z = wrap(z + d, 8)
+                send(remote(zb.at[to_z], zr.at[z], zss.at[d - 1], zrs.at[d - 1], at(dz=d)))
+    zr[z] = zb[z]
+
     def share(n, d, arrivals):
         for k in arrivals:
             wait_h(0, k)
@@ -328,13 +328,8 @@
         ref = TT.at[wrap(x + d, 4), 1 - c]
         remote(ref, ref, us.at[n], ur.at[n], at(dc=1)).wait_recv()
 
+    shared(0, 0)
     arrange(x)
-    share(1, -1, (1,))
-    share(2, 1, (3,))
-    shared(1, -1)
-    arrange(wrap(x - 1, 4))
-    shared(2, 1)
-    arrange(wrap(x + 1, 4))
     for d in (1, 2, 3):
         ref = PR.at[wrap(x - d, 4)]
         remote(ref, ref, ps.at[d - 1], prs.at[d - 1], at(dx=d)).wait_recv()
@@ -354,56 +349,74 @@
 
     for i in range(4):
         span = slice(32 * i, 32 * i + 32)
-        W[y, zl, span] = low_teacher(group[span], *[PR[i, k, 0:32] for k in range(3)]).astype(BF16)
-    first_row = iota((8, 256), 0) == 0
+        W[h, y, zl, span] = low_teacher(group[span], *[PR[i, k, 0:32] for k in range(3)]).astype(BF16)
+    first_row = iota((8, 128), 0) == 0
     extras = [jnp.where(first_row, PR[x, k, 32:40], PR[3, k, 32:40]) for k in range(3)]
     block = low_teacher(group[128:136], *extras)
-    block = jnp.where(iota((8, 256), 0) < 3, block, 0.0)
-    W[y, zl, 128:144] = jnp.concatenate([block, jnp.zeros((8, 256), F32)], axis=0).astype(BF16)
+    block = jnp.where(iota((8, 128), 0) < 3, block, 0.0)
+    W[h, y, zl, 128:144] = jnp.concatenate([block, jnp.zeros((8, 128), F32)], axis=0).astype(BF16)
 
     parts = [pl.ds(0, 80), pl.ds(80, 64)]
-    layers = [zl, wrap(zl - 1, 4), wrap(zl + 1, 4), wrap(zl + 2, 4)]
-    spread_w, wait_w, relay_w = ring(
-        lambda n, d, half: W.at[wrap(y + d, 4), layers[n], half], parts, along_y, w3s, w3r
-    )
-    for k, (ref, d) in enumerate(
-        [(W.at[y, zl], 1), (W.at[y, zl], -1), (W.at[y, zl, parts[0]], 2), (W.at[y, zl, parts[1]], -2)]
-    ):
-        send(remote(ref, ref, w2s.at[k], w2r.at[k], at(dz=d)))
+    away = [0, -1, 1, -2, 2, -3, 3, 4]
+
+    def block_of(n, d, half=None):
+        owner = wrap(z + away[n], 8)
+        ref = W.at[lax.div(owner, 4), wrap(y + d, 4), lax.rem(owner, 4)]
+        return ref if half is None else ref.at[half]
+
+    spread_w, wait_w, relay_w = ring(block_of, parts, along_y, w3s, w3r)
+    own = block_of(0, 0)
+    for n in range(1, 8):
+        send(remote(own, own, w2s.at[n - 1], w2r.at[n - 1], at(dz=-away[n])))
     spread_w(0)
 
+    both[h] = group[0:136]
+    twin = remote(both.at[h], both.at[h], hs.at[0], hr.at[0], at(dz=4))
+    send(twin)
+
+    def follow(n):
+        ref = block_of(n, 0)
+        remote(ref, ref, w2s.at[n - 1], w2r.at[n - 1], at(dz=-away[n])).wait_recv()
+        spread_w(n)
+        relay_w(n - 1)
+
+    share(1, -1, (1,))
+    share(2, 1, (3,))
+    follow(1)
+    follow(2)
+    follow(3)
+    follow(4)
+    shared(1, -1)
+    arrange(wrap(x - 1, 4))
+    follow(5)
+    follow(6)
+    follow(7)
+
+    ref = both.at[1 - h]
+    remote(ref, ref, hs.at[0], hr.at[0], at(dz=4)).wait_recv()
     for i in range(4):
-        xs[i, 0:32] = group[32 * i : 32 * i + 32]
-        xs[i, 32:40] = group[128:136]
+        for k in range(2):
+            side = slice(128 * k, 128 * k + 128)
+            xs[i, 0:32, side] = both[k, 32 * i : 32 * i + 32]
+            xs[i, 32:40, side] = both[k, 128:136]
     slot = 2 * x + c
     others = [(dx, dc) for dx in range(4) for dc in range(2) if dx or dc]
     for n, (dx, dc) in enumerate(others):
         send(remote(xs.at[wrap(x + dx, 4)], xr.at[slot], xss.at[n], xrs.at[n], at(dx=dx, dc=dc)))
     xr[slot] = xs[x]
-
-    for n, k in ((1, 0), (2, 1)):
-        ref = W.at[y, layers[n]]
-        remote(ref, ref, w2s.at[k], w2r.at[k], at(dz=1)).wait_recv()
-        spread_w(n)
-    for k in (2, 3):
-        ref = W.at[y, layers[3], parts[k - 2]]
-        remote(ref, ref, w2s.at[k], w2r.at[k], at(dz=1)).wait_recv()
-    spread_w(3)
-    relay_w(0)
     share(3, 2, (4, 5))
-    relay_w(1)
-    relay_w(2)
+    relay_w(7)
+    shared(2, 1)
+    arrange(wrap(x + 1, 4))
 
     def accumulate(i, a):
         total = jnp.zeros((256, 256), F32)
-        for h in range(2):
-            right = W[i, 2 * h : 2 * h + 2, 0:128].reshape(256, 256)
-            total += jnp.dot(TP[2 * i + h, a], right, preferred_element_type=F32)
+        for k in range(2):
+            sides = [W[n, i, 2 * k : 2 * k + 2, 0:128].reshape(256, 128) for n in range(2)]
+            right = jnp.concatenate(sides, axis=1)
+            total += jnp.dot(TP[2 * i + k, a], right, preferred_element_type=F32)
         return total
 
-    relay_w(3)
-    shared(3, 2)
-    arrange(wrap(x + 2, 4))
 
     for n, (dx, dc) in enumerate(others):
         ref = xr.at[2 * wrap(x - dx, 4) + wrap(c - dc, 2)]
@@ -457,13 +470,16 @@
     for copy in results:
         copy.start()
 
+    shared(3, 2)
+    arrange(wrap(x + 2, 4))
+
     def begin(a, carry):
         acc[a] = accumulate(y, a)
         return carry
 
     lax.fori_loop(0, 4, begin, 0)
     for d, arrivals in ((-1, (1,)), (1, (3,)), (2, (4, 5))):
-        for n in range(4):
+        for n in range(8):
             for k in arrivals:
                 wait_w(n, k)
         if d != 2:
@@ -474,9 +490,9 @@
 
             lax.fori_loop(0, 4, more, 0)
 
-    bias_t = W[3, 3, 128:144].astype(F32)[1:2]
-    scale_t = W[3, 3, 128:144].astype(F32)[2:3]
-    ends = W[:, :, 128:144].reshape(256, 256)
+    ends = jnp.concatenate([W[n, :, :, 128:144].reshape(256, 128) for n in range(2)], axis=1)
+    tail = ends[240:256].astype(F32)
+    bias_t, scale_t = tail[1:2], tail[2:3]
     out_cols = branch_res.at[:, pl.ds(pl.multiple_of(256 * slot, 128), 256)]
     n = 0
     for d in (2, 1, 3, 0):
@@ -541,10 +557,11 @@
             pltpu.VMEM((528, 512), F32),
             pltpu.VMEM((4, GROUP, 512), BF16),
             pltpu.VMEM((4, GROUP, 256), BF16),
-            pltpu.VMEM((4, GROUP, 256), BF16),
-            pltpu.VMEM((8, GROUP, 256), BF16),
-            pltpu.VMEM((4, 3, 40, 256), F32),
-            pltpu.VMEM((4, 3, 40, 256), F32),
+            pltpu.VMEM((8, GROUP, 128), BF16),
+            pltpu.VMEM((8, GROUP, 128), BF16),
+            pltpu.VMEM((4, 3, 40, 128), F32),
+            pltpu.VMEM((4, 3, 40, 128), F32),
+            pltpu.VMEM((2, 136, 128), F32),
             pltpu.VMEM((4, 40, 256), F32),
             pltpu.VMEM((8, 40, 256), F32),
             pltpu.VMEM((256, 128), F32),
@@ -553,15 +570,16 @@
             pltpu.VMEM((8, 384, 384), BF16),
             pltpu.VMEM((8, 4, 256, 256), BF16),
             pltpu.VMEM((4, 256, 256), BF16),
-            pltpu.VMEM((4, 4, GROUP, 256), BF16),
+            pltpu.VMEM((2, 4, 4, GROUP, 128), BF16),
             pltpu.VMEM((4, 256, 256), F32),
             pltpu.VMEM((4, 2, 128, 256), BF16),
             dma((9,)), dma((4,)), dma((2,)),
             dma((3,)), dma((3,)), dma((3,)), dma((3,)), dma((3,)), dma((3,)), dma((3,)), dma((3,)),
             dma((4, 6)), dma((4, 6)), dma((4, 6)), dma((4, 6)),
-            dma((1,)), dma((1,)), dma((7,)), dma((7,)),
+            dma((4,)), dma((4,)), dma((7,)), dma((7,)),
             dma((3,)), dma((3,)), dma((7,)), dma((7,)),
-            dma((1, 6)), dma((1, 6)), dma((4,)), dma((4,)), dma((4,)), dma((4,)), dma((4, 6)), dma((4, 6)),
+            dma((1, 6)), dma((1, 6)), dma((4,)), dma((4,)), dma((7,)), dma((7,)), dma((8, 6)), dma((8, 6)),
+            dma((1,)), dma((1,)),
             dma((7,)), dma((8,)),
         ],
         compiler_params=pltpu.CompilerParams(collective_id=0, has_side_effects=True, vmem_limit_bytes=56 << 20),

time: 91.2 us -> 96.6 us (1.059)
  Pallas kernels: 90.4 us -> 95.9 us
    pallas_call x1, Pallas kernels: 88.2 us -> 93.6 us  [per_device(): pl.pallas_call(kernel, out_shape=results, in_specs=[pl.BlockSpec(memory_s...]
where the time goes in v5:
time: 96.6 us; the launch traced here: 96.5 us
  Pallas kernels  95.9 us (99%)
    pallas_call x1, Pallas kernels, per_device(): pl.pallas_call(kernel, out_shape=results, in_specs=[pl.BlockSpec(memory_s...  93.6 us
    pallas_call x1, Pallas kernels, per_device(): pl.pallas_call(copy_kernel, out_shape=results, in_specs=[anyspace] * 5, o...  2.24 us

profile of v5, /device:TPU:1, one launch (start us, length us, event | category | flops | bytes accessed | tf_op | source)
XLA Modules:
  0.0 96.5 jit_solution(5557523797328529004)
XLA Ops:
  0.6 93.6 %step.1 = (f32[516,128]{1,0:T(8,128)}, f32[516,128]{1,0:T(8,128)}, f32[516,128]{1,0:T(8,128)}, f32[516,128]{1,0:T(8,128)}, bf16[128,2048]{1,0:T(8,128)(2,1)}) custom-call(s32[3]{0:T(128)} %offsets.1, f32[1,2048]{1,0:T(1,128)} %bitcast.13, bf16[128,2048]{1,0:T(8,128)(2,1)} %tokens_hbm.1, bf16[128,2048]{1,0:T(8,128)(2,1)} %cot_hbm.1, ...), custom_call_target="tpu_custom_call" | custom-call | tf_op jit(solution)/shard_map/step/pallas_call | solution.py:542
  94.3 2.2 %place.1 = (f32[516,128]{1,0:T(8,128)}, f32[516,128]{1,0:T(8,128)}, f32[516,128]{1,0:T(8,128)}, f32[516,128]{1,0:T(8,128)}, bf16[128,2048]{1,0:T(8,128)(2,1)}) custom-call(f32[516,128]{1,0:T(8,128)} %get-tuple-element.15.refs_0_, f32[516,128]{1,0:T(8,128)} %get-tuple-element.16.refs_1_, f32[516,128]{1,0:T(8,128)} %get-tuple-element.17.refs_2_, ...), custom_call_target="tpu_custom_call" | custom-call | tf_op jit(solution)/shard_map/place/pallas_call | solution.py:591

commit v6 on v5

--- a/solution.py
+++ b/solution.py
@@ -56,7 +56,7 @@
     gain, tok, cot, saved, master, one, two, teacher, mix, master_out, one_out, two_out, teacher_out,
     TW, T, C, SX, SL, SS, prod, zs, cr, zb, zr, PS, PR, both, xs, xr, pad, tg, TT, S, TP, TE, W, acc, OUT,
     in_sem, res_sem, own_sem, a1s, a1r, b1s, b1r, s1s, s1r, s2s, s2r, a2s, a2r, b2s, b2r, cs, crs, zss, zrs,
-    ps, prs, xss, xrs, ts, tr, us, ur, w2s, w2r, w3s, w3r, hs, hr, os, orr,
+    ps, prs, xss, xrs, ts, tr, us, ur, w2s, w2r, w3s, w3r, hs, hr, fs, fr, os, orr,
 ):
     f = lax.axis_index("fsdp")
     p = lax.axis_index("dp")
@@ -80,7 +80,7 @@
         pltpu.make_async_copy(src, dst, in_sem.at[k])
         for k, (src, dst) in enumerate(
             [
-                (tokens_hbm, tok), (cot_hbm, cot), (saved_hbm, saved), (tt_hbm, TT.at[x, c]), (gain_hbm, gain),
+                (tokens_hbm, tok), (cot_hbm, cot), (saved_hbm, saved), (tt_hbm, TT.at[0, c]), (gain_hbm, gain),
                 (master_hbm, master), (one_hbm, one), (two_hbm, two), (teacher_hbm, teacher),
             ]
         )
@@ -98,45 +98,43 @@
         copy.start()
         pending.append(copy)
 
-    def ring(view, halves, to, sends, recvs):
+    def settle(copies):
+        for copy in copies:
+            copy.wait_send()
+
+    def ring(view, to, sends, recvs):
         def spread(n):
             for k, (half, d) in enumerate([(0, 1), (1, 1), (1, -1), (0, -1)]):
-                ref = view(n, 0, halves[half])
-                send(remote(ref, ref, sends.at[n, k], recvs.at[n, k], to(d)))
+                send(remote(view(n, 0, half), view(n, -d % 4, half), sends.at[n, k], recvs.at[n, k], to(d)))
 
         def wait(n, k):
-            half, d = [(0, -1), (1, -1), (1, 1), (0, 1), (0, -2), (1, 2)][k]
-            ref = view(n, d, halves[half])
+            half, d = [(0, 3), (1, 3), (1, 1), (0, 1), (0, 2), (1, 2)][k]
+            ref = view(n, d, half)
             remote(ref, ref, sends.at[n, k], recvs.at[n, k], to(1)).wait_recv()
-            return ref
 
         def relay(n):
-            for k, d in ((0, 1), (2, -1)):
-                ref = wait(n, k)
-                send(remote(ref, ref, sends.at[n, 4 + k // 2], recvs.at[n, 4 + k // 2], to(d)))
+            for k, half, d in ((0, 0, 1), (2, 1, -1)):
+                wait(n, k)
+                j = 4 + k // 2
+                send(remote(view(n, -d % 4, half), view(n, 2, half), sends.at[n, j], recvs.at[n, j], to(d)))
 
         return spread, wait, relay
 
     halves = [pl.ds(0, 64), pl.ds(64, 64)]
+    groups = [pl.ds(0, 1), pl.ds(1, 3)]
     along_x = lambda d: at(dx=d)
     along_y = lambda d: at(dy=d)
-    spread_t, wait_t, relay_t = ring(
-        lambda n, d, half: T.at[wrap(y - n, 4), wrap(x + d, 4), half], halves, along_x, a2s, a2r
-    )
-    spread_c, wait_c, relay_c = ring(
-        lambda n, d, half: C.at[wrap(y + d, 4), wrap(x - n, 4), half], halves, along_y, b2s, b2r
-    )
-    spread_h, wait_h, relay_h = ring(
-        lambda n, d, half: TT.at[wrap(x + d, 4), c, half], halves, along_x, ts, tr
-    )
+    spread_t, wait_t, relay_t = ring(lambda n, d, k: T.at[d, groups[n], halves[k]], along_x, a2s, a2r)
+    spread_c, wait_c, relay_c = ring(lambda n, d, k: C.at[groups[n], d, halves[k]], along_y, b2s, b2r)
+    spread_h, wait_h, relay_h = ring(lambda n, d, k: TT.at[d, c, halves[k]], along_x, ts, tr)
 
     def quarter(i):
         return cot_hbm.at[:, pl.ds(pl.multiple_of(512 * i, 128), 512)]
 
-    mine = pltpu.make_async_copy(quarter(x), C.at[y, x], own_sem.at[0])
+    mine = pltpu.make_async_copy(quarter(x), C.at[0, 0], own_sem.at[0])
     mine.start()
     for d in (1, 2, 3):
-        send(remote(quarter(wrap(x + d, 4)), C.at[y, x], b1s.at[d - 1], b1r.at[d - 1], at(dx=d)))
+        send(remote(quarter(wrap(x + d, 4)), C.at[4 - d, 0], b1s.at[d - 1], b1r.at[d - 1], at(dx=d)))
     loads[0].wait()
     for i in range(4):
         end = min(512 * i + 640, WIDTH)
@@ -149,13 +147,13 @@
             window = jnp.where(iota((128, 512), 1) < 500, window, 0.0)
         TW[i] = window.astype(BF16)
     for d in (1, 2, 3):
-        send(remote(TW.at[wrap(y + d, 4)], T.at[y, x], a1s.at[d - 1], a1r.at[d - 1], at(dy=d)))
-    T[y, x] = TW[y]
+        send(remote(TW.at[wrap(y + d, 4)], T.at[0, 4 - d], a1s.at[d - 1], a1r.at[d - 1], at(dy=d)))
+    T[0, 0] = TW[y]
     spread_t(0)
     mine.wait()
     spread_c(0)
     loads[3].wait()
-    send(remote(TT.at[x, c], TT.at[x, c], us.at[0], ur.at[0], at(dc=1)))
+    send(remote(TT.at[0, c], TT.at[0, c], us.at[0], ur.at[0], at(dc=1)))
     loads[1].wait()
     loads[2].wait()
     total = jnp.zeros((1, WIDTH), F32)
@@ -179,15 +177,16 @@
         send(remote(SS.at[wrap(x + d, 4)], SX.at[x], s1s.at[d - 1], s1r.at[d - 1], at(dx=d)))
     SX[x] = SS[x]
 
-    for d, before in ((1, 0), (3, 1), (2, 3)):
-        ref = T.at[wrap(y - d, 4), x]
+    for d in (1, 2, 3):
+        ref = T.at[0, 4 - d]
         remote(ref, ref, a1s.at[d - 1], a1r.at[d - 1], at(dy=d)).wait_recv()
-        spread_t(d)
-        ref = C.at[y, wrap(x - d, 4)]
+    spread_t(1)
+    for d in (1, 2, 3):
+        ref = C.at[4 - d, 0]
         remote(ref, ref, b1s.at[d - 1], b1r.at[d - 1], at(dx=d)).wait_recv()
-        spread_c(d)
-        relay_t(before)
-        relay_c(before)
+    spread_c(1)
+    relay_t(0)
+    relay_c(0)
 
     for d in (1, 2, 3):
         ref = SX.at[wrap(x - d, 4)]
@@ -219,22 +218,25 @@
         for b in range(4):
             for m in range(4):
                 four = [source[pl.ds(128 * b + 4 * m + t, 8, stride=16), :] for t in range(4)]
-                PS[wrap(x + m, 4), k, 8 * b : 8 * b + 8] = mine_of(four)
+                PS[m, k, 8 * b : 8 * b + 8] = mine_of(four)
         tail = source[TAIL : TAIL + 256]
         moved = roll_by(tail, row_back, 0, range(7, 15))[0:24]
         rolled = roll_by(moved, lane_back, 1, range(7))
         bias = jnp.where(lanes24 < 128 - lane_at, rolled, pltpu.roll(rolled, 23, 0))
         for m in range(4):
-            PS[m, k, 32:33] = mine_of([source[512 + t : 513 + t] for t in range(4)])
-            PS[m, k, 33:34] = mine_of([bias[4 * m + t : 4 * m + t + 1] for t in range(4)])
-            PS[m, k, 34:35] = mine_of([tail[240 + 4 * m + t : 241 + 4 * m + t] for t in range(4)])
-            PS[m, k, 35:40] = jnp.zeros((5, 128), F32)
-
-    relay_t(2)
-    relay_c(2)
-    for d in (1, 2, 3):
-        send(remote(PS.at[wrap(x + d, 4)], PR.at[x], ps.at[d - 1], prs.at[d - 1], at(dx=d)))
-    PR[x] = PS[x]
+            to = wrap(m - x, 4)
+            PS[to, k, 32:33] = mine_of([source[512 + t : 513 + t] for t in range(4)])
+            PS[to, k, 33:34] = mine_of([bias[4 * m + t : 4 * m + t + 1] for t in range(4)])
+            PS[to, k, 34:35] = mine_of([tail[240 + 4 * m + t : 241 + 4 * m + t] for t in range(4)])
+            PS[to, k, 35:40] = jnp.zeros((5, 128), F32)
+
+    relay_t(1)
+    relay_c(1)
+    plane = list(pending)
+    pending.clear()
+    for d in (1, 2, 3):
+        send(remote(PS.at[d], PR.at[4 - d], ps.at[d - 1], prs.at[d - 1], at(dx=d)))
+    PR[0] = PS[0]
     spread_h(0)
 
     def one_hot(g, carry):
@@ -264,18 +266,18 @@
 
     ones = jnp.ones((16, 512), BF16)
     cot_sum = jnp.zeros((16, 512), F32)
-    for n, arrivals in ((0, ()), (1, (1,)), (3, (3,)), (2, (4, 5))):
-        for k in (1, 3, 4, 5):
-            wait_t(n, k)
+    for step, (i, arrivals) in enumerate(((0, ()), (3, (1,)), (1, (3,)), (2, (4, 5)))):
+        if not step:
+            for n in range(2):
+                for k in (1, 3, 4, 5):
+                    wait_t(n, k)
         for k in arrivals:
-            for i in range(4):
-                wait_c(i, k)
-        row = wrap(y - n, 4)
-        right = C[row].reshape(512, 512)
-        part = lax.dot_general(
-            T[row].reshape(512, 512), right, (((0,), (0,)), ((), ())), preferred_element_type=F32
-        )
-        if n:
+            for n in range(2):
+                wait_c(n, k)
+        right = C[:, i].reshape(512, 512)
+        left = T[:, i].reshape(512, 512)
+        part = lax.dot_general(left, right, (((0,), (0,)), ((), ())), preferred_element_type=F32)
+        if step:
             prod[0:512] += part
         else:
             prod[0:512] = part
@@ -321,17 +323,18 @@
     def share(n, d, arrivals):
         for k in arrivals:
             wait_h(0, k)
-        ref = TT.at[wrap(x + d, 4), c]
+        ref = TT.at[d, c]
         send(remote(ref, ref, us.at[n], ur.at[n], at(dc=1)))
 
     def shared(n, d):
-        ref = TT.at[wrap(x + d, 4), 1 - c]
+        ref = TT.at[d, 1 - c]
         remote(ref, ref, us.at[n], ur.at[n], at(dc=1)).wait_recv()
 
     shared(0, 0)
-    arrange(x)
-    for d in (1, 2, 3):
-        ref = PR.at[wrap(x - d, 4)]
+    arrange(0)
+    settle(plane)
+    for d in (1, 2, 3):
+        ref = PR.at[4 - d]
         remote(ref, ref, ps.at[d - 1], prs.at[d - 1], at(dx=d)).wait_recv()
     for d in range(1, 8):
         ref = zr.at[wrap(z - d, 8)]
@@ -349,48 +352,53 @@
 
     for i in range(4):
         span = slice(32 * i, 32 * i + 32)
-        W[h, y, zl, span] = low_teacher(group[span], *[PR[i, k, 0:32] for k in range(3)]).astype(BF16)
+        W[0, 0, span] = low_teacher(group[span], *[PR[wrap(i - x, 4), k, 0:32] for k in range(3)]).astype(BF16)
     first_row = iota((8, 128), 0) == 0
-    extras = [jnp.where(first_row, PR[x, k, 32:40], PR[3, k, 32:40]) for k in range(3)]
+    extras = [jnp.where(first_row, PR[0, k, 32:40], PR[wrap(3 - x, 4), k, 32:40]) for k in range(3)]
     block = low_teacher(group[128:136], *extras)
     block = jnp.where(iota((8, 128), 0) < 3, block, 0.0)
-    W[h, y, zl, 128:144] = jnp.concatenate([block, jnp.zeros((8, 128), F32)], axis=0).astype(BF16)
-
+    W[0, 0, 128:144] = jnp.concatenate([block, jnp.zeros((8, 128), F32)], axis=0).astype(BF16)
+
+    before_columns = list(pending)
+    pending.clear()
     parts = [pl.ds(0, 80), pl.ds(80, 64)]
-    away = [0, -1, 1, -2, 2, -3, 3, 4]
-
-    def block_of(n, d, half=None):
-        owner = wrap(z + away[n], 8)
-        ref = W.at[lax.div(owner, 4), wrap(y + d, 4), lax.rem(owner, 4)]
-        return ref if half is None else ref.at[half]
-
-    spread_w, wait_w, relay_w = ring(block_of, parts, along_y, w3s, w3r)
-    own = block_of(0, 0)
-    for n in range(1, 8):
-        send(remote(own, own, w2s.at[n - 1], w2r.at[n - 1], at(dz=-away[n])))
+
+    def column_view(n, d, k):
+        if n == 0:
+            return W.at[d, 0, parts[k]]
+        return W.at[d, (1 if n == 1 else 6) + k]
+
+    spread_w, wait_w, relay_w = ring(column_view, along_y, w3s, w3r)
+    for d in (4, 1, 7, 2, 6, 3, 5):
+        send(remote(W.at[0, 0], W.at[0, 8 - d], w2s.at[d - 1], w2r.at[d - 1], at(dz=d)))
     spread_w(0)
 
     both[h] = group[0:136]
     twin = remote(both.at[h], both.at[h], hs.at[0], hr.at[0], at(dz=4))
     send(twin)
 
-    def follow(n):
-        ref = block_of(n, 0)
-        remote(ref, ref, w2s.at[n - 1], w2r.at[n - 1], at(dz=-away[n])).wait_recv()
-        spread_w(n)
-        relay_w(n - 1)
-
-    share(1, -1, (1,))
+    def come(d):
+        ref = W.at[0, 8 - d]
+        remote(ref, ref, w2s.at[d - 1], w2r.at[d - 1], at(dz=d)).wait_recv()
+
+    share(1, 3, (1,))
     share(2, 1, (3,))
-    follow(1)
-    follow(2)
-    follow(3)
-    follow(4)
-    shared(1, -1)
-    arrange(wrap(x - 1, 4))
-    follow(5)
-    follow(6)
-    follow(7)
+    come(7)
+    come(6)
+    spread_w(1)
+    come(1)
+    come(2)
+    spread_w(2)
+    relay_w(0)
+    for d in (3, 5, 4):
+        come(d)
+    far = W.at[0, pl.ds(3, 3)]
+    for d in (1, 2, 3):
+        send(remote(far, W.at[4 - d, pl.ds(3, 3)], fs.at[d - 1], fr.at[d - 1], at(dy=d)))
+    relay_w(1)
+    relay_w(2)
+    shared(1, 3)
+    arrange(3)
 
     ref = both.at[1 - h]
     remote(ref, ref, hs.at[0], hr.at[0], at(dz=4)).wait_recv()
@@ -405,18 +413,73 @@
         send(remote(xs.at[wrap(x + dx, 4)], xr.at[slot], xss.at[n], xrs.at[n], at(dx=dx, dc=dc)))
     xr[slot] = xs[x]
     share(3, 2, (4, 5))
-    relay_w(7)
     shared(2, 1)
-    arrange(wrap(x + 1, 4))
+    arrange(1)
+
+    def block_at(i, j, n):
+        return W.at[i, wrap(4 * n + j - z, 8)]
 
     def accumulate(i, a):
         total = jnp.zeros((256, 256), F32)
         for k in range(2):
-            sides = [W[n, i, 2 * k : 2 * k + 2, 0:128].reshape(256, 128) for n in range(2)]
+            sides = [
+                jnp.concatenate([block_at(i, 2 * k + j, n)[0:128] for j in range(2)], axis=0) for n in range(2)
+            ]
             right = jnp.concatenate(sides, axis=1)
-            total += jnp.dot(TP[2 * i + k, a], right, preferred_element_type=F32)
+            total += jnp.dot(TP[2 * wrap(y + i, 4) + k, a], right, preferred_element_type=F32)
         return total
 
+    shared(3, 2)
+    arrange(2)
+    settle(before_columns)
+
+    def add(i, fresh):
+        def body(a, carry):
+            if fresh:
+                acc[a] = accumulate(i, a)
+            else:
+                acc[a] += accumulate(i, a)
+            return carry
+
+        lax.fori_loop(0, 4, body, 0)
+
+    add(0, True)
+    for i, arrivals in ((3, (1,)), (1, (3,)), (2, (4, 5))):
+        for n in range(3):
+            for k in arrivals:
+                wait_w(n, k)
+        ref = W.at[i, pl.ds(3, 3)]
+        remote(ref, ref, fs.at[0], fr.at[3 - i], at(dy=1)).wait_recv()
+        if i != 2:
+            add(i, False)
+
+    ends = jnp.concatenate(
+        [
+            jnp.concatenate(
+                [block_at(wrap(i - y, 4), j, n)[128:144] for i in range(4) for j in range(4)], axis=0
+            )
+            for n in range(2)
+        ],
+        axis=1,
+    )
+    tail = ends[240:256].astype(F32)
+    bias_t, scale_t = tail[1:2], tail[2:3]
+    columns = list(pending)
+    pending.clear()
+    out_cols = branch_res.at[:, pl.ds(pl.multiple_of(256 * slot, 128), 256)]
+    n = 0
+    for d in (2, 1, 3, 0):
+        a = d
+        total = acc[a] + accumulate(2, a) + jnp.dot(TE[a], ends, preferred_element_type=F32)
+        OUT[a] = (scale_t * (total + bias_t)).astype(BF16).reshape(2, 128, 256)
+        for dc in range(2):
+            core = wrap(c + dc, 2)
+            if d or dc:
+                send(remote(OUT.at[a, core], out_cols, os.at[n], orr.at[slot], at(dx=d, dc=dc)))
+                n += 1
+    stay = pltpu.make_async_copy(OUT.at[0, c], out_cols, own_sem.at[1])
+    stay.start()
+    settle(columns)
 
     for n, (dx, dc) in enumerate(others):
         ref = xr.at[2 * wrap(x - dx, 4) + wrap(c - dc, 2)]
@@ -470,42 +533,6 @@
     for copy in results:
         copy.start()
 
-    shared(3, 2)
-    arrange(wrap(x + 2, 4))
-
-    def begin(a, carry):
-        acc[a] = accumulate(y, a)
-        return carry
-
-    lax.fori_loop(0, 4, begin, 0)
-    for d, arrivals in ((-1, (1,)), (1, (3,)), (2, (4, 5))):
-        for n in range(8):
-            for k in arrivals:
-                wait_w(n, k)
-        if d != 2:
-
-            def more(a, carry):
-                acc[a] += accumulate(wrap(y + d, 4), a)
-                return carry
-
-            lax.fori_loop(0, 4, more, 0)
-
-    ends = jnp.concatenate([W[n, :, :, 128:144].reshape(256, 128) for n in range(2)], axis=1)
-    tail = ends[240:256].astype(F32)
-    bias_t, scale_t = tail[1:2], tail[2:3]
-    out_cols = branch_res.at[:, pl.ds(pl.multiple_of(256 * slot, 128), 256)]
-    n = 0
-    for d in (2, 1, 3, 0):
-        a = wrap(x + d, 4)
-        total = acc[a] + accumulate(wrap(y + 2, 4), a) + jnp.dot(TE[a], ends, preferred_element_type=F32)
-        OUT[a] = (scale_t * (total + bias_t)).astype(BF16).reshape(2, 128, 256)
-        for dc in range(2):
-            core = wrap(c + dc, 2)
-            if d or dc:
-                send(remote(OUT.at[a, core], out_cols, os.at[n], orr.at[slot], at(dx=d, dc=dc)))
-                n += 1
-    stay = pltpu.make_async_copy(OUT.at[x, c], out_cols, own_sem.at[1])
-    stay.start()
     for n, (dx, dc) in enumerate(others):
         e = 2 * wrap(x - dx, 4) + wrap(c - dc, 2)
         ref = branch_res.at[:, pl.ds(pl.multiple_of(256 * e, 128), 256)]
@@ -513,8 +540,7 @@
     stay.wait()
     for copy in results:
         copy.wait()
-    for copy in pending:
-        copy.wait_send()
+    settle(pending)
 
 
 def copy_kernel(*refs):
@@ -570,16 +596,16 @@
             pltpu.VMEM((8, 384, 384), BF16),
             pltpu.VMEM((8, 4, 256, 256), BF16),
             pltpu.VMEM((4, 256, 256), BF16),
-            pltpu.VMEM((2, 4, 4, GROUP, 128), BF16),
+            pltpu.VMEM((4, 8, GROUP, 128), BF16),
             pltpu.VMEM((4, 256, 256), F32),
             pltpu.VMEM((4, 2, 128, 256), BF16),
             dma((9,)), dma((4,)), dma((2,)),
             dma((3,)), dma((3,)), dma((3,)), dma((3,)), dma((3,)), dma((3,)), dma((3,)), dma((3,)),
-            dma((4, 6)), dma((4, 6)), dma((4, 6)), dma((4, 6)),
+            dma((2, 6)), dma((2, 6)), dma((2, 6)), dma((2, 6)),
             dma((4,)), dma((4,)), dma((7,)), dma((7,)),
             dma((3,)), dma((3,)), dma((7,)), dma((7,)),
-            dma((1, 6)), dma((1, 6)), dma((4,)), dma((4,)), dma((7,)), dma((7,)), dma((8, 6)), dma((8, 6)),
-            dma((1,)), dma((1,)),
+            dma((1, 6)), dma((1, 6)), dma((4,)), dma((4,)), dma((7,)), dma((7,)), dma((3, 6)), dma((3, 6)),
+            dma((1,)), dma((1,)), dma((3,)), dma((3,)),
             dma((7,)), dma((8,)),
         ],
         compiler_params=pltpu.CompilerParams(collective_id=0, has_side_effects=True, vmem_limit_bytes=56 << 20),

time: 96.6 us -> 88.4 us (0.915)
  Pallas kernels: 95.9 us -> 87.6 us
    pallas_call x1, Pallas kernels: 93.6 us -> 85.4 us  [per_device(): pl.pallas_call(kernel, out_shape=results, in_specs=[pl.BlockSpec(memory_s...]
where the time goes in v6:
time: 88.4 us; the launch traced here: 88.3 us
  Pallas kernels  87.6 us (99%)
    pallas_call x1, Pallas kernels, per_device(): pl.pallas_call(kernel, out_shape=results, in_specs=[pl.BlockSpec(memory_s...  85.4 us
    pallas_call x1, Pallas kernels, per_device(): pl.pallas_call(copy_kernel, out_shape=results, in_specs=[anyspace] * 5, o...  2.24 us

profile of v6, /device:TPU:1, one launch (start us, length us, event | category | flops | bytes accessed | tf_op | source)
XLA Modules:
  0.0 88.3 jit_solution(4998247927469854321)
XLA Ops:
  0.6 85.4 %step.1 = (f32[516,128]{1,0:T(8,128)}, f32[516,128]{1,0:T(8,128)}, f32[516,128]{1,0:T(8,128)}, f32[516,128]{1,0:T(8,128)}, bf16[128,2048]{1,0:T(8,128)(2,1)}) custom-call(s32[3]{0:T(128)} %offsets.1, f32[1,2048]{1,0:T(1,128)} %bitcast.13, bf16[128,2048]{1,0:T(8,128)(2,1)} %tokens_hbm.1, bf16[128,2048]{1,0:T(8,128)(2,1)} %cot_hbm.1, ...), custom_call_target="tpu_custom_call" | custom-call | tf_op jit(solution)/shard_map/step/pallas_call | solution.py:568
  86.0 2.2 %place.1 = (f32[516,128]{1,0:T(8,128)}, f32[516,128]{1,0:T(8,128)}, f32[516,128]{1,0:T(8,128)}, f32[516,128]{1,0:T(8,128)}, bf16[128,2048]{1,0:T(8,128)(2,1)}) custom-call(f32[516,128]{1,0:T(8,128)} %get-tuple-element.15.refs_0_, f32[516,128]{1,0:T(8,128)} %get-tuple-element.16.refs_1_, f32[516,128]{1,0:T(8,128)} %get-tuple-element.17.refs_2_, ...), custom_call_target="tpu_custom_call" | custom-call | tf_op jit(solution)/shard_map/place/pallas_call | solution.py:617

commit v7 on v6

--- a/solution.py
+++ b/solution.py
@@ -53,8 +53,8 @@
 def kernel(
     offsets, gain_hbm, tokens_hbm, cot_hbm, saved_hbm, master_hbm, one_hbm, two_hbm, teacher_hbm, tt_hbm,
     master_res, one_res, two_res, teacher_res, branch_res,
-    gain, tok, cot, saved, master, one, two, teacher, mix, master_out, one_out, two_out, teacher_out,
-    TW, T, C, SX, SL, SS, prod, zs, cr, zb, zr, PS, PR, both, xs, xr, pad, tg, TT, S, TP, TE, W, acc, OUT,
+    gain, tok, cot, saved, raw, master, one, two, teacher, mix, master_out, one_out, two_out, teacher_out,
+    TW, T, C, SX, SL, SS, prod, zs, cr, zb, zr, PS, PR, both, xs, xr, pad, tg, TT, W, acc, OUT,
     in_sem, res_sem, own_sem, a1s, a1r, b1s, b1r, s1s, s1r, s2s, s2r, a2s, a2r, b2s, b2r, cs, crs, zss, zrs,
     ps, prs, xss, xrs, ts, tr, us, ur, w2s, w2r, w3s, w3r, hs, hr, fs, fr, os, orr,
 ):
@@ -80,7 +80,7 @@
         pltpu.make_async_copy(src, dst, in_sem.at[k])
         for k, (src, dst) in enumerate(
             [
-                (tokens_hbm, tok), (cot_hbm, cot), (saved_hbm, saved), (tt_hbm, TT.at[0, c]), (gain_hbm, gain),
+                (tokens_hbm, tok), (cot_hbm, cot), (saved_hbm, saved), (tt_hbm, raw), (gain_hbm, gain),
                 (master_hbm, master), (one_hbm, one), (two_hbm, two), (teacher_hbm, teacher),
             ]
         )
@@ -135,6 +135,8 @@
     mine.start()
     for d in (1, 2, 3):
         send(remote(quarter(wrap(x + d, 4)), C.at[4 - d, 0], b1s.at[d - 1], b1r.at[d - 1], at(dx=d)))
+    mine.wait()
+    spread_c(0)
     loads[0].wait()
     for i in range(4):
         end = min(512 * i + 640, WIDTH)
@@ -150,10 +152,6 @@
         send(remote(TW.at[wrap(y + d, 4)], T.at[0, 4 - d], a1s.at[d - 1], a1r.at[d - 1], at(dy=d)))
     T[0, 0] = TW[y]
     spread_t(0)
-    mine.wait()
-    spread_c(0)
-    loads[3].wait()
-    send(remote(TT.at[0, c], TT.at[0, c], us.at[0], ur.at[0], at(dc=1)))
     loads[1].wait()
     loads[2].wait()
     total = jnp.zeros((1, WIDTH), F32)
@@ -230,6 +228,26 @@
             PS[to, k, 34:35] = mine_of([tail[240 + 4 * m + t : 241 + 4 * m + t] for t in range(4)])
             PS[to, k, 35:40] = jnp.zeros((5, 128), F32)
 
+    loads[3].wait()
+
+    def arrange(g, extra):
+        for k in range(2):
+            j = 2 * g + k
+            start = pl.multiple_of(jnp.minimum(128 * j, WIDTH - 256), 128)
+            col = iota((1, 256), 1)
+            lane = lax.rem(col, 128)
+            source = jnp.where(col < 128, 129 * j + lane, jnp.where(lane == 16 * lax.rem(j, 8), 129 * j + 128, -1))
+            pick = jnp.where(iota((256, 256), 0) == source - start, 1.0, 0.0).astype(BF16)
+            part = jnp.dot(raw[:, pl.ds(start, 256)], pick, preferred_element_type=F32)
+            TT[0, c, :, pl.ds(pl.multiple_of(128 * j, 128), 128)] = part[:, :128].astype(BF16)
+            extra += part[:, 128:]
+        return extra
+
+    for half in range(2):
+        extra = lax.fori_loop(4 * half, 4 * half + 4, arrange, jnp.zeros((128, 128), F32))
+        TT[0, c, :, WIDTH + 128 * half : WIDTH + 128 * half + 128] = extra.astype(BF16)
+    send(remote(TT.at[0, c], TT.at[0, c], us.at[0], ur.at[0], at(dc=1)))
+
     relay_t(1)
     relay_c(1)
     plane = list(pending)
@@ -239,30 +257,15 @@
     PR[0] = PS[0]
     spread_h(0)
 
-    def one_hot(g, carry):
-        col = iota((1, 384), 1)
-        i = lax.div(lax.rem(col, 128), 32)
-        source = 258 * g + lax.div(col, 128) * 129 + lax.rem(col, 128) + jnp.where(i > x, 1, 0)
-        slot = lax.rem(col, 128) - 32 * lax.rem(g, 4)
-        extra = 258 * g + 32 * x + 32 + jnp.where(slot == 0, 0, 129)
-        extra = jnp.where(jnp.logical_or(slot == 0, slot == 16), extra, -1)
-        source = jnp.where(col < 256, source, extra) - jnp.minimum(256 * g, WIDTH - 384)
-        S[g] = jnp.where(iota((384, 384), 0) == source, 1.0, 0.0).astype(BF16)
-        return carry
-
-    lax.fori_loop(0, 8, one_hot, 0)
-
-    def arrange(a):
-        def group(g, extra):
-            start = pl.multiple_of(jnp.minimum(256 * g, WIDTH - 384), 128)
-            block = TT[a, :, :, pl.ds(start, 384)].reshape(256, 384)
-            part = jnp.dot(block, S[g], preferred_element_type=F32)
-            TP[g, a] = part[:, :256].astype(BF16)
-            return extra + part[:, 256:]
-
-        for h in range(2):
-            extra = lax.fori_loop(4 * h, 4 * h + 4, group, jnp.zeros((256, 128), F32))
-            TE[a, :, 128 * h : 128 * h + 128] = extra.astype(BF16)
+    def share(n, d, arrivals):
+        for k in arrivals:
+            wait_h(0, k)
+        ref = TT.at[d, c]
+        send(remote(ref, ref, us.at[n], ur.at[n], at(dc=1)))
+
+    def shared(n, d):
+        ref = TT.at[d, 1 - c]
+        remote(ref, ref, us.at[n], ur.at[n], at(dc=1)).wait_recv()
 
     ones = jnp.ones((16, 512), BF16)
     cot_sum = jnp.zeros((16, 512), F32)
@@ -320,18 +323,6 @@
                 send(remote(zb.at[to_z], zr.at[z], zss.at[d - 1], zrs.at[d - 1], at(dz=d)))
     zr[z] = zb[z]
 
-    def share(n, d, arrivals):
-        for k in arrivals:
-            wait_h(0, k)
-        ref = TT.at[d, c]
-        send(remote(ref, ref, us.at[n], ur.at[n], at(dc=1)))
-
-    def shared(n, d):
-        ref = TT.at[d, 1 - c]
-        remote(ref, ref, us.at[n], ur.at[n], at(dc=1)).wait_recv()
-
-    shared(0, 0)
-    arrange(0)
     settle(plane)
     for d in (1, 2, 3):
         ref = PR.at[4 - d]
@@ -350,14 +341,18 @@
         second = new_two / (1.0 - beta_two**STEP)
         return mixed - ((1.0 - ema_rate) * learn_rate) * (first / (jnp.sqrt(second) + epsilon))
 
-    for i in range(4):
-        span = slice(32 * i, 32 * i + 32)
-        W[0, 0, span] = low_teacher(group[span], *[PR[wrap(i - x, 4), k, 0:32] for k in range(3)]).astype(BF16)
+    main = [low_teacher(group[32 * i : 32 * i + 32], *[PR[wrap(i - x, 4), k, 0:32] for k in range(3)]) for i in range(4)]
     first_row = iota((8, 128), 0) == 0
     extras = [jnp.where(first_row, PR[0, k, 32:40], PR[wrap(3 - x, 4), k, 32:40]) for k in range(3)]
     block = low_teacher(group[128:136], *extras)
-    block = jnp.where(iota((8, 128), 0) < 3, block, 0.0)
-    W[0, 0, 128:144] = jnp.concatenate([block, jnp.zeros((8, 128), F32)], axis=0).astype(BF16)
+    nothing = jnp.zeros((8, 128), F32)
+    plain = jnp.concatenate(main + [nothing, nothing], axis=0)
+    moved = pltpu.roll(plain, 1, 0)
+    at_row = iota((GROUP, 128), 0)
+    place_row = 32 * x + 32
+    plain = jnp.where(at_row < place_row, plain, jnp.where(at_row == place_row, block[0:1], moved))
+    plain = jnp.where(at_row == 129, block[1:2], jnp.where(at_row == 130, block[2:3], plain))
+    W[0, 0] = plain.astype(BF16)
 
     before_columns = list(pending)
     pending.clear()
@@ -381,8 +376,6 @@
         ref = W.at[0, 8 - d]
         remote(ref, ref, w2s.at[d - 1], w2r.at[d - 1], at(dz=d)).wait_recv()
 
-    share(1, 3, (1,))
-    share(2, 1, (3,))
     come(7)
     come(6)
     spread_w(1)
@@ -390,6 +383,8 @@
     come(2)
     spread_w(2)
     relay_w(0)
+    share(1, 3, (1,))
+    share(2, 1, (3,))
     for d in (3, 5, 4):
         come(d)
     far = W.at[0, pl.ds(3, 3)]
@@ -397,8 +392,6 @@
         send(remote(far, W.at[4 - d, pl.ds(3, 3)], fs.at[d - 1], fr.at[d - 1], at(dy=d)))
     relay_w(1)
     relay_w(2)
-    shared(1, 3)
-    arrange(3)
 
     ref = both.at[1 - h]
     remote(ref, ref, hs.at[0], hr.at[0], at(dz=4)).wait_recv()
@@ -413,8 +406,6 @@
         send(remote(xs.at[wrap(x + dx, 4)], xr.at[slot], xss.at[n], xrs.at[n], at(dx=dx, dc=dc)))
     xr[slot] = xs[x]
     share(3, 2, (4, 5))
-    shared(2, 1)
-    arrange(1)
 
     def block_at(i, j, n):
         return W.at[i, wrap(4 * n + j - z, 8)]
@@ -426,11 +417,15 @@
                 jnp.concatenate([block_at(i, 2 * k + j, n)[0:128] for j in range(2)], axis=0) for n in range(2)
             ]
             right = jnp.concatenate(sides, axis=1)
-            total += jnp.dot(TP[2 * wrap(y + i, 4) + k, a], right, preferred_element_type=F32)
+            start = pl.multiple_of(512 * wrap(y + i, 4) + 256 * k, 128)
+            left = TT[a, :, :, pl.ds(start, 256)].reshape(256, 256)
+            total += jnp.dot(left, right, preferred_element_type=F32)
         return total
 
+    shared(0, 0)
+    shared(1, 3)
+    shared(2, 1)
     shared(3, 2)
-    arrange(2)
     settle(before_columns)
 
     def add(i, fresh):
@@ -470,7 +465,9 @@
     n = 0
     for d in (2, 1, 3, 0):
         a = d
-        total = acc[a] + accumulate(2, a) + jnp.dot(TE[a], ends, preferred_element_type=F32)
+        total = acc[a] + accumulate(2, a) + jnp.dot(
+            TT[a, :, :, WIDTH:].reshape(256, 256), ends, preferred_element_type=F32
+        )
         OUT[a] = (scale_t * (total + bias_t)).astype(BF16).reshape(2, 128, 256)
         for dc in range(2):
             core = wrap(c + dc, 2)
@@ -572,7 +569,7 @@
         out_specs=[anyspace] * 5,
         scratch_shapes=[
             pltpu.VMEM((1, WIDTH), F32),
-            rows, rows, rows,
+            rows, rows, rows, rows,
             shard, shard, shard, shard, shard, shard, shard, shard, shard,
             pltpu.VMEM((4, 128, 512), BF16),
             pltpu.VMEM((4, 4, 128, 512), BF16),
@@ -592,10 +589,7 @@
             pltpu.VMEM((8, 40, 256), F32),
             pltpu.VMEM((256, 128), F32),
             pltpu.VMEM((520, 128), F32),
-            pltpu.VMEM((4, 2, 128, WIDTH), BF16),
-            pltpu.VMEM((8, 384, 384), BF16),
-            pltpu.VMEM((8, 4, 256, 256), BF16),
-            pltpu.VMEM((4, 256, 256), BF16),
+            pltpu.VMEM((4, 2, 128, WIDTH + 256), BF16),
             pltpu.VMEM((4, 8, GROUP, 128), BF16),
             pltpu.VMEM((4, 256, 256), F32),
             pltpu.VMEM((4, 2, 128, 256), BF16),

time: 88.4 us -> 85.1 us (0.963)
  Pallas kernels: 87.6 us -> 84.4 us
    pallas_call x1, Pallas kernels: 85.4 us -> 82.1 us  [per_device(): pl.pallas_call(kernel, out_shape=results, in_specs=[pl.BlockSpec(memory_s...]
where the time goes in v7:
time: 85.1 us; the launch traced here: 85 us
  Pallas kernels  84.4 us (99%)
    pallas_call x1, Pallas kernels, per_device(): pl.pallas_call(kernel, out_shape=results, in_specs=[pl.BlockSpec(memory_s...  82.1 us
    pallas_call x1, Pallas kernels, per_device(): pl.pallas_call(copy_kernel, out_shape=results, in_specs=[anyspace] * 5, o...  2.24 us

profile of v7, /device:TPU:1, one launch (start us, length us, event | category | flops | bytes accessed | tf_op | source)
XLA Modules:
  0.0 85.0 jit_solution(7466407837423775545)
XLA Ops:
  0.6 82.1 %step.1 = (f32[516,128]{1,0:T(8,128)}, f32[516,128]{1,0:T(8,128)}, f32[516,128]{1,0:T(8,128)}, f32[516,128]{1,0:T(8,128)}, bf16[128,2048]{1,0:T(8,128)(2,1)}) custom-call(s32[3]{0:T(128)} %offsets.1, f32[1,2048]{1,0:T(1,128)} %bitcast.13, bf16[128,2048]{1,0:T(8,128)(2,1)} %tokens_hbm.1, bf16[128,2048]{1,0:T(8,128)(2,1)} %cot_hbm.1, ...), custom_call_target="tpu_custom_call" | custom-call | tf_op jit(solution)/shard_map/step/pallas_call | solution.py:565
  82.8 2.2 %place.1 = (f32[516,128]{1,0:T(8,128)}, f32[516,128]{1,0:T(8,128)}, f32[516,128]{1,0:T(8,128)}, f32[516,128]{1,0:T(8,128)}, bf16[128,2048]{1,0:T(8,128)(2,1)}) custom-call(f32[516,128]{1,0:T(8,128)} %get-tuple-element.15.refs_0_, f32[516,128]{1,0:T(8,128)} %get-tuple-element.16.refs_1_, f32[516,128]{1,0:T(8,128)} %get-tuple-element.17.refs_2_, ...), custom_call_target="tpu_custom_call" | custom-call | tf_op jit(solution)/shard_map/place/pallas_call | solution.py:611

commit v8 on v7

--- a/solution.py
+++ b/solution.py
@@ -428,25 +428,17 @@
     shared(3, 2)
     settle(before_columns)
 
-    def add(i, fresh):
-        def body(a, carry):
-            if fresh:
-                acc[a] = accumulate(i, a)
-            else:
-                acc[a] += accumulate(i, a)
-            return carry
-
-        lax.fori_loop(0, 4, body, 0)
-
-    add(0, True)
+    def begin(a, carry):
+        acc[a] = accumulate(0, a)
+        return carry
+
+    lax.fori_loop(0, 4, begin, 0)
     for i, arrivals in ((3, (1,)), (1, (3,)), (2, (4, 5))):
         for n in range(3):
             for k in arrivals:
                 wait_w(n, k)
         ref = W.at[i, pl.ds(3, 3)]
         remote(ref, ref, fs.at[0], fr.at[3 - i], at(dy=1)).wait_recv()
-        if i != 2:
-            add(i, False)
 
     ends = jnp.concatenate(
         [
@@ -465,7 +457,7 @@
     n = 0
     for d in (2, 1, 3, 0):
         a = d
-        total = acc[a] + accumulate(2, a) + jnp.dot(
+        total = acc[a] + accumulate(3, a) + accumulate(1, a) + accumulate(2, a) + jnp.dot(
             TT[a, :, :, WIDTH:].reshape(256, 256), ends, preferred_element_type=F32
         )
         OUT[a] = (scale_t * (total + bias_t)).astype(BF16).reshape(2, 128, 256)

time: 85.1 us -> 83.4 us (0.980)
  Pallas kernels: 84.4 us -> 82.6 us
    pallas_call x1, Pallas kernels: 82.1 us -> 80.4 us  [per_device(): pl.pallas_call(kernel, out_shape=results, in_specs=[pl.BlockSpec(memory_s...]
where the time goes in v8:
time: 83.4 us; the launch traced here: 83.3 us
  Pallas kernels  82.6 us (99%)
    pallas_call x1, Pallas kernels, per_device(): pl.pallas_call(kernel, out_shape=results, in_specs=[pl.BlockSpec(memory_s...  80.4 us
    pallas_call x1, Pallas kernels, per_device(): pl.pallas_call(copy_kernel, out_shape=results, in_specs=[anyspace] * 5, o...  2.24 us

profile of v8, /device:TPU:1, one launch (start us, length us, event | category | flops | bytes accessed | tf_op | source)
XLA Modules:
  0.0 83.3 jit_solution(8199659397467905485)
XLA Ops:
  0.6 80.4 %step.1 = (f32[516,128]{1,0:T(8,128)}, f32[516,128]{1,0:T(8,128)}, f32[516,128]{1,0:T(8,128)}, f32[516,128]{1,0:T(8,128)}, bf16[128,2048]{1,0:T(8,128)(2,1)}) custom-call(s32[3]{0:T(128)} %offsets.1, f32[1,2048]{1,0:T(1,128)} %bitcast.13, bf16[128,2048]{1,0:T(8,128)(2,1)} %tokens_hbm.1, bf16[128,2048]{1,0:T(8,128)(2,1)} %cot_hbm.1, ...), custom_call_target="tpu_custom_call" | custom-call | tf_op jit(solution)/shard_map/step/pallas_call | solution.py:557
  81.0 2.2 %place.1 = (f32[516,128]{1,0:T(8,128)}, f32[516,128]{1,0:T(8,128)}, f32[516,128]{1,0:T(8,128)}, f32[516,128]{1,0:T(8,128)}, bf16[128,2048]{1,0:T(8,128)(2,1)}) custom-call(f32[516,128]{1,0:T(8,128)} %get-tuple-element.15.refs_0_, f32[516,128]{1,0:T(8,128)} %get-tuple-element.16.refs_1_, f32[516,128]{1,0:T(8,128)} %get-tuple-element.17.refs_2_, ...), custom_call_target="tpu_custom_call" | custom-call | tf_op jit(solution)/shard_map/place/pallas_call | solution.py:603

commit v9 on v8

--- a/solution.py
+++ b/solution.py
@@ -267,24 +267,24 @@
         ref = TT.at[d, 1 - c]
         remote(ref, ref, us.at[n], ur.at[n], at(dc=1)).wait_recv()
 
-    ones = jnp.ones((16, 512), BF16)
-    cot_sum = jnp.zeros((16, 512), F32)
-    for step, (i, arrivals) in enumerate(((0, ()), (3, (1,)), (1, (3,)), (2, (4, 5)))):
-        if not step:
-            for n in range(2):
-                for k in (1, 3, 4, 5):
-                    wait_t(n, k)
-        for k in arrivals:
-            for n in range(2):
-                wait_c(n, k)
-        right = C[:, i].reshape(512, 512)
-        left = T[:, i].reshape(512, 512)
+    def multiply(spots):
+        left = jnp.concatenate([T[i, k].reshape(-1, 512) for i, k in spots], axis=0)
+        right = jnp.concatenate([C[i, k].reshape(-1, 512) for i, k in spots], axis=0)
         part = lax.dot_general(left, right, (((0,), (0,)), ((), ())), preferred_element_type=F32)
-        if step:
-            prod[0:512] += part
-        else:
-            prod[0:512] = part
-        cot_sum += jnp.dot(ones, right, preferred_element_type=F32)
+        return part, jnp.dot(jnp.ones((16, right.shape[0]), BF16), right, preferred_element_type=F32)
+
+    for n in range(2):
+        for k in (1, 3):
+            wait_t(n, k)
+            wait_c(n, k)
+    prod[0:512], cot_sum = multiply([(slice(0, 2), k) for k in (0, 1, 3)] + [(3, k) for k in (0, 1, 3)])
+    for n in range(2):
+        for k in (4, 5):
+            wait_t(n, k)
+            wait_c(n, k)
+    part, more = multiply([(2, slice(0, 4)), (slice(0, 2), 2), (3, 2)])
+    prod[0:512] += part
+    cot_sum += more
 
     small = SL[y].astype(F32)
     for d in (1, 2, 3):
@@ -461,7 +461,7 @@
             TT[a, :, :, WIDTH:].reshape(256, 256), ends, preferred_element_type=F32
         )
         OUT[a] = (scale_t * (total + bias_t)).astype(BF16).reshape(2, 128, 256)
-        for dc in range(2):
+        for dc in (1, 0):
             core = wrap(c + dc, 2)
             if d or dc:
                 send(remote(OUT.at[a, core], out_cols, os.at[n], orr.at[slot], at(dx=d, dc=dc)))

time: 83.4 us -> 83 us (level)
  no operation moved by 1% of the time
where the time goes in v9:
time: 83 us; the launch traced here: 82.6 us
  Pallas kernels  81.9 us (99%)
    pallas_call x1, Pallas kernels, per_device(): pl.pallas_call(kernel, out_shape=results, in_specs=[pl.BlockSpec(memory_s...  79.7 us
    pallas_call x1, Pallas kernels, per_device(): pl.pallas_call(copy_kernel, out_shape=results, in_specs=[anyspace] * 5, o...  2.24 us

profile of v9, /device:TPU:1, one launch (start us, length us, event | category | flops | bytes accessed | tf_op | source)
XLA Modules:
  0.0 82.6 jit_solution(9691024378306151921)
XLA Ops:
  0.6 79.7 %step.1 = (f32[516,128]{1,0:T(8,128)}, f32[516,128]{1,0:T(8,128)}, f32[516,128]{1,0:T(8,128)}, f32[516,128]{1,0:T(8,128)}, bf16[128,2048]{1,0:T(8,128)(2,1)}) custom-call(s32[3]{0:T(128)} %offsets.1, f32[1,2048]{1,0:T(1,128)} %bitcast.13, bf16[128,2048]{1,0:T(8,128)(2,1)} %tokens_hbm.1, bf16[128,2048]{1,0:T(8,128)(2,1)} %cot_hbm.1, ...), custom_call_target="tpu_custom_call" | custom-call | tf_op jit(solution)/shard_map/step/pallas_call | solution.py:557
  80.3 2.2 %place.1 = (f32[516,128]{1,0:T(8,128)}, f32[516,128]{1,0:T(8,128)}, f32[516,128]{1,0:T(8,128)}, f32[516,128]{1,0:T(8,128)}, bf16[128,2048]{1,0:T(8,128)(2,1)}) custom-call(f32[516,128]{1,0:T(8,128)} %get-tuple-element.15.refs_0_, f32[516,128]{1,0:T(8,128)} %get-tuple-element.16.refs_1_, f32[516,128]{1,0:T(8,128)} %get-tuple-element.17.refs_2_, ...), custom_call_target="tpu_custom_call" | custom-call | tf_op jit(solution)/shard_map/place/pallas_call | solution.py:603

commit v10 on v9

--- a/solution.py
+++ b/solution.py
@@ -385,13 +385,14 @@
     relay_w(0)
     share(1, 3, (1,))
     share(2, 1, (3,))
-    for d in (3, 5, 4):
-        come(d)
-    far = W.at[0, pl.ds(3, 3)]
-    for d in (1, 2, 3):
-        send(remote(far, W.at[4 - d, pl.ds(3, 3)], fs.at[d - 1], fr.at[d - 1], at(dy=d)))
-    relay_w(1)
-    relay_w(2)
+    for n, group in enumerate(((3, 5), (4,))):
+        for d in group:
+            come(d)
+        for d in (1, 2, 3):
+            for i in group:
+                j = (3, 5, 4).index(i)
+                send(remote(W.at[0, 8 - i], W.at[4 - d, 8 - i], fs.at[j, d - 1], fr.at[j, d - 1], at(dy=d)))
+        relay_w(1 + n)
 
     ref = both.at[1 - h]
     remote(ref, ref, hs.at[0], hr.at[0], at(dz=4)).wait_recv()
@@ -437,8 +438,9 @@
         for n in range(3):
             for k in arrivals:
                 wait_w(n, k)
-        ref = W.at[i, pl.ds(3, 3)]
-        remote(ref, ref, fs.at[0], fr.at[3 - i], at(dy=1)).wait_recv()
+        for j in range(3):
+            ref = W.at[i, (5, 3, 4)[j]]
+            remote(ref, ref, fs.at[j, 0], fr.at[j, 3 - i], at(dy=1)).wait_recv()
 
     ends = jnp.concatenate(
         [
@@ -591,7 +593,7 @@
             dma((4,)), dma((4,)), dma((7,)), dma((7,)),
             dma((3,)), dma((3,)), dma((7,)), dma((7,)),
             dma((1, 6)), dma((1, 6)), dma((4,)), dma((4,)), dma((7,)), dma((7,)), dma((3, 6)), dma((3, 6)),
-            dma((1,)), dma((1,)), dma((3,)), dma((3,)),
+            dma((1,)), dma((1,)), dma((3, 3)), dma((3, 3)),
             dma((7,)), dma((8,)),
         ],
         compiler_params=pltpu.CompilerParams(collective_id=0, has_side_effects=True, vmem_limit_bytes=56 << 20),

time: 83 us -> 83 us (level)
  no operation moved by 1% of the time
where the time goes in v10:
time: 83 us; the launch traced here: 82.7 us
  Pallas kernels  82.1 us (99%)
    pallas_call x1, Pallas kernels, per_device(): pl.pallas_call(kernel, out_shape=results, in_specs=[pl.BlockSpec(memory_s...  79.8 us
    pallas_call x1, Pallas kernels, per_device(): pl.pallas_call(copy_kernel, out_shape=results, in_specs=[anyspace] * 5, o...  2.24 us

profile of v10, /device:TPU:1, one launch (start us, length us, event | category | flops | bytes accessed | tf_op | source)
XLA Modules:
  0.0 82.7 jit_solution(17640255681710602232)
XLA Ops:
  0.6 79.8 %step.1 = (f32[516,128]{1,0:T(8,128)}, f32[516,128]{1,0:T(8,128)}, f32[516,128]{1,0:T(8,128)}, f32[516,128]{1,0:T(8,128)}, bf16[128,2048]{1,0:T(8,128)(2,1)}) custom-call(s32[3]{0:T(128)} %offsets.1, f32[1,2048]{1,0:T(1,128)} %bitcast.13, bf16[128,2048]{1,0:T(8,128)(2,1)} %tokens_hbm.1, bf16[128,2048]{1,0:T(8,128)(2,1)} %cot_hbm.1, ...), custom_call_target="tpu_custom_call" | custom-call | tf_op jit(solution)/shard_map/step/pallas_call | solution.py:559
  80.5 2.2 %place.1 = (f32[516,128]{1,0:T(8,128)}, f32[516,128]{1,0:T(8,128)}, f32[516,128]{1,0:T(8,128)}, f32[516,128]{1,0:T(8,128)}, bf16[128,2048]{1,0:T(8,128)(2,1)}) custom-call(f32[516,128]{1,0:T(8,128)} %get-tuple-element.15.refs_0_, f32[516,128]{1,0:T(8,128)} %get-tuple-element.16.refs_1_, f32[516,128]{1,0:T(8,128)} %get-tuple-element.17.refs_2_, ...), custom_call_target="tpu_custom_call" | custom-call | tf_op jit(solution)/shard_map/place/pallas_call | solution.py:605
